TPU v7x, 512 devices: a whole 4x4x16 slice. The times are simulated.
512 devices in a mesh: dp: 32 (over y, z_lo), mp: 16 (over x, z_hi, core).
Axes of the slice: x: 4, y: 4, z: 16 (z_hi: 2, z_lo: 8; z = z_hi * 8 + z_lo), core: 2. Of those that a mesh axis runs over, the one named last changes fastest.
Arguments:
- tokens: bfloat16 [4096, 6144], P('dp', 'mp'), as said below
- norm_gain: bfloat16 [6144], P('mp'), may hold values from 0.099609375 to 1.8984375
- attn_weights: bfloat16 [4, 6144, 4096], P(None, 'dp', 'mp'), as said below
- stored_grads: bfloat16 [4, 6144, 4096], P(None, 'dp', 'mp'), as said below
- cotangent: bfloat16 [4096, 6144], P('dp'), may hold values from -12 to 12
Outputs:
- input_grad: bfloat16 [4096, 6144], P('dp', 'mp')
Inputs may be any that keep to these rules, and one draw needn't show every extreme that they name: `tokens`: Real-valued. `attn_weights`: Real-valued. `stored_grads`: Real-valued.
All inputs are finite; a program needn't handle non-finite values.
Results may differ from a plain program's by a relative error of at most 0.024.
Values may be sent and summed in bfloat16 or wider, within the bound.
A program may use at most 128 MiB of HBM per device.

v0:
```python
import jax
import jax.numpy as jnp
from jax import lax
from jax.sharding import PartitionSpec as P

HD = 128
PATCHES = 128


ascent_radius = 0.15


def row_norm(matrix):
    center = matrix - jnp.mean(matrix, axis=-1, keepdims=True)
    inverse = lax.rsqrt(jnp.mean(center * center, axis=-1, keepdims=True) + 1e-06)
    return (center * inverse, inverse)


def row_norm_back(upstream, normed, inverse):
    first_mean = jnp.mean(upstream, axis=-1, keepdims=True)
    second_mean = jnp.mean(upstream * normed, axis=-1, keepdims=True)
    return (upstream - first_mean - normed * second_mean) * inverse


def per_device(tokens, norm_gain, attn_weights, stored_grads, cotangent):
    weight_squares = jnp.sum(jnp.square(attn_weights.astype(jnp.float32)), axis=(1, 2))
    grad_squares = jnp.sum(jnp.square(stored_grads.astype(jnp.float32)), axis=(1, 2))
    weight_squares, grad_squares = lax.psum((weight_squares, grad_squares), ("dp", "mp"))
    ascent_ratio = ascent_radius * jnp.sqrt(weight_squares) / (jnp.sqrt(grad_squares) + 1e-12)
    shifted = (
        attn_weights.astype(jnp.float32)
        + ascent_ratio[:, None, None] * stored_grads.astype(jnp.float32)
    ).astype(jnp.bfloat16)
    full_rows, full_gain = (
        lax.all_gather(tokens, "mp", axis=1, tiled=True),
        lax.all_gather(norm_gain.reshape(1, -1), "mp", axis=1, tiled=True),
    )
    normed, inverse = row_norm(full_rows.astype(jnp.float32))
    gain_row = full_gain.astype(jnp.float32)
    normed_in = (normed * gain_row).astype(jnp.bfloat16)
    gathered = lax.all_gather(shifted, "dp", axis=1, tiled=True)
    project = gathered[:3]
    out_proj = gathered[3]
    tokens_here = full_rows.shape[0]
    width = project.shape[2]
    head_count = width // HD
    images = tokens_here // PATCHES
    head_shape = (images, PATCHES, head_count, HD)
    score_scale = HD ** (-0.5)
    projected = jnp.einsum("td,mde->mte", normed_in, project, preferred_element_type=jnp.float32)
    q_hat, q_inv = row_norm(projected[0].reshape(head_shape))
    k_hat, k_inv = row_norm(projected[1].reshape(head_shape))
    queries = q_hat.astype(jnp.bfloat16)
    key_rows = k_hat.astype(jnp.bfloat16)
    value_rows = projected[2].reshape(head_shape).astype(jnp.bfloat16)
    scores = (
        jnp.einsum("bqhe,bkhe->bhqk", queries, key_rows, preferred_element_type=jnp.float32)
        * score_scale
    )
    exps = jnp.exp(scores)
    probabilities = exps / jnp.sum(exps, axis=-1, keepdims=True)
    grad_attn = jnp.dot(cotangent, out_proj, preferred_element_type=jnp.float32).astype(
        jnp.bfloat16
    )
    grad_attn = grad_attn.reshape(head_shape)
    probs_low = probabilities.astype(jnp.bfloat16)
    grad_values = jnp.einsum(
        "bhqk,bqhe->bkhe", probs_low, grad_attn, preferred_element_type=jnp.float32
    )
    grad_probs = jnp.einsum(
        "bqhe,bkhe->bhqk", grad_attn, value_rows, preferred_element_type=jnp.float32
    )
    inner = jnp.sum(probabilities * grad_probs, axis=-1, keepdims=True)
    grad_scores = (probabilities * (grad_probs - inner) * score_scale).astype(jnp.bfloat16)
    grad_query = jnp.einsum(
        "bhqk,bkhe->bqhe", grad_scores, key_rows, preferred_element_type=jnp.float32
    )
    grad_keys = jnp.einsum(
        "bhqk,bqhe->bkhe", grad_scores, queries, preferred_element_type=jnp.float32
    )
    grad_q = (
        row_norm_back(grad_query, q_hat, q_inv).astype(jnp.bfloat16).reshape(tokens_here, width)
    )
    grad_k = row_norm_back(grad_keys, k_hat, k_inv).astype(jnp.bfloat16).reshape(tokens_here, width)
    grad_v = grad_values.astype(jnp.bfloat16).reshape(tokens_here, width)
    stacked = jnp.stack([grad_q, grad_k, grad_v])
    term = jnp.einsum("mte,mde->td", stacked, project, preferred_element_type=jnp.float32)
    width_all = term.shape[1]
    share_width = width_all // lax.axis_size("mp")
    offset = lax.axis_index("mp") * share_width
    normed_share = lax.dynamic_slice_in_dim(normed, offset, share_width, 1)
    gain_share = norm_gain.astype(jnp.float32)[None, :]
    share_sum = lax.psum_scatter(
        term.astype(jnp.bfloat16), "mp", scatter_dimension=1, tiled=True
    ).astype(jnp.float32)
    upstream = share_sum * gain_share
    first_sum, second_sum = lax.psum(
        (jnp.sum(upstream, axis=-1), jnp.sum(upstream * normed_share, axis=-1)), "mp"
    )
    result = (
        upstream - first_sum[:, None] / width_all - normed_share * second_sum[:, None] / width_all
    ) * inverse
    return result.astype(jnp.bfloat16)


def solution(mesh):
    return jax.shard_map(
        per_device,
        mesh=mesh,
        in_specs=(P("dp", "mp"), P("mp"), P(None, "dp", "mp"), P(None, "dp", "mp"), P("dp", None)),
        out_specs=P("dp", "mp"),
        check_vma=False,
    )
```

profile of v0, /device:TPU:7, one launch (start us, length us, event | category | flops | bytes accessed | tf_op | source)
XLA Modules:
  0.0 651.1 jit_solution(13680243375521069659)
XLA Ops:
  6.5 0.0 copy-start
  6.5 0.0 copy-start.4
  6.5 0.0 all-gather.7.cloned.1.call-start
  6.5 0.7 all-gather.7.cloned.1.call-update
  7.3 0.0 all-gather.5.cloned.1.call-start
  7.3 1.4 fusion.19
  8.7 120.4 %all-reduce = (f32[4]{0:T(128)S(1)}, f32[4]{0:T(128)S(1)}) all-reduce(f32[4]{0:T(128)S(1)} %get-tuple-element.22, f32[4]{0:T(128)S(1)} %get-tuple-element.21), channel_id=1, replica_groups=mesh['dp'=32,'mp'=16] {'dp','mp'}, use_global_device_ids=true, to_apply=%region_3.0 | all-reduce | flops 8 | bytes 64 | tf_op jit(solution)/shard_map/psum | solution.py:28
  129.1 1.3 fusion.20
  130.5 1.1 copy.48
  131.6 0.0 all-gather.5.cloned.1.call-update
  131.6 0.0 reduce-scatter.4.cloned.1.call-start
  131.6 0.0 copy-done.4
  131.7 39.9 %all-gather.1 = bf16[16,1,384]{2,1,0:T(2,128)(2,1)S(1)} all-gather(bf16[1,1,384]{2,1,0:T(2,128)(2,1)S(1)} %reshape.232), channel_id=2, replica_groups=mesh['dp'=32,'mp'=16] {'mp'}, dimensions={0}, use_global_device_ids=true | all-gather | bytes 13056 | tf_op jit(solution)/shard_map/all_gather | solution.py:36
  171.6 0.0 all-gather.7.cloned.1.call-done
  171.6 1.7 convert_reduce_fusion
  173.4 0.0 copy-start.8
  173.4 2.0 fusion.4
  175.4 0.0 copy-start.6
  175.4 242.2 %all-gather.5.cloned.1.call-done = bf16[4,6144,256]{2,0,1:T(4,128)(2,1)} async-done(((bf16[4,192,256]{2,0,1:T(4,128)(2,1)}), bf16[4,6144,256]{2,0,1:T(4,128)(2,1)}) %all-gather.5.cloned.1.call-update) | async-done | bytes 12582928 | tf_op jit(solution)/shard_map/all_gather | solution.py:41
  417.5 0.0 copy-start.1
  417.5 19.1 %copy.72 = bf16[3,6144,256]{1,2,0:T(8,128)(2,1)} copy(bf16[3,6144,256]{2,0,1:T(4,128)(2,1)} %bitcast.53) | data formatting | bytes 18874368
  436.7 0.0 copy-done.8
  436.7 0.0 copy-done.6
  436.7 0.0 copy-done.1
  436.7 5.3 fusion.10
  442.0 0.0 copy-start.2
  442.0 0.7 copy-done.2
  443.0 0.2 fusion.14
  443.2 0.0 copy-start.3
  443.2 0.6 copy-done.3
  443.9 0.7 fusion.34
  444.6 8.6 %slice.24 = bf16[1,6144,256]{2,0,1:T(2,128)(2,1)S(1)} slice(bf16[4,6144,256]{2,0,1:T(4,128)(2,1)} %all-gather.5.cloned.1.call-done), slice={[3:4], [0:6144], [0:256]} | slice | bytes 6291456 | tf_op jit(solution)/shard_map/slice | solution.py:43
  453.2 0.0 copy-done
  453.2 1.1 fusion.18
  454.3 1.8 convolution_convert_fusion
  456.1 0.9 fusion.51
  457.0 1.9 fusion.44
  458.9 2.5 fusion.45
  461.4 0.9 copy.60
  462.3 0.7 broadcast_multiply_fusion.1
  463.0 0.7 broadcast_multiply_fusion.3
  463.7 0.7 broadcast_multiply_fusion.2
  464.3 0.7 broadcast_multiply_fusion
  465.0 1.1 multiply_convert_fusion.3
  466.1 0.1 copy.58
  466.2 0.1 copy.59
  466.3 6.2 fusion.1
  472.6 0.0 copy-start.5
  472.6 0.0 copy-start.7
  472.6 0.0 copy-start.9
  472.6 2.6 copy.70
  475.2 0.0 reduce-scatter.4.cloned.1.call-update
  475.2 0.0 copy-done.5
  475.2 0.0 copy-done.7
  475.2 0.0 copy-done.9
  475.2 2.2 fusion.2
  477.4 104.2 %reduce-scatter.4.cloned.1.call-done = bf16[384,128]{1,0:T(8,128)(2,1)} async-done(((bf16[6144,128]{1,0:T(8,128)(2,1)}), bf16[384,128]{1,0:T(8,128)(2,1)}) %reduce-scatter.4.cloned.1.call-update) | async-done | bytes 98320
  581.7 1.0 copy.71
  582.7 1.0 fusion.31
  583.7 59.1 %all-reduce.1 = (f32[128]{0:T(128)S(1)}, f32[128]{0:T(128)S(1)}) all-reduce(f32[128]{0:T(128)S(1)} %get-tuple-element.10, f32[128]{0:T(128)S(1)} %get-tuple-element.9), channel_id=1, replica_groups=mesh['dp'=32,'mp'=16] {'mp'}, use_global_device_ids=true, to_apply=%region_20.0 | all-reduce | flops 256 | bytes 2048 | tf_op jit(solution)/shard_map/psum | solution.py:97
  642.9 1.7 multiply_convert_fusion.1
  (17 shorter events, 0.2 us)
Async XLA Ops:
  6.5 446.6 %copy-start = (bf16[128,6144]{1,0:T(8,128)(2,1)S(1)}, bf16[128,6144]{1,0:T(8,128)(2,1)}, u32[]{:S(2)}) copy-start(bf16[128,6144]{1,0:T(8,128)(2,1)} %param.9) | copy-start | bytes 4718596
  6.5 125.1 %copy-start.4 = (bf16[384]{0:T(512)(128)(2,1)S(1)}, bf16[384]{0:T(512)(128)(2,1)}, u32[]{:S(2)}) copy-start(bf16[384]{0:T(512)(128)(2,1)} %param.6) | copy-start | bytes 2308
  6.5 165.1 %all-gather.7.cloned.1.call-start = ((), (), s32[]{:S(2)}) async-start(), calls=%async_computation.2 | async-start | bytes 1671168 | tf_op jit(solution)/shard_map/all_gather | solution.py:35
  7.3 410.3 %all-gather.5.cloned.1.call-start = ((), (), s32[]{:S(2)}) async-start(), calls=%async_computation.1 | async-start | bytes 12976128 | tf_op jit(solution)/shard_map/all_gather | solution.py:41
  131.6 450.1 %reduce-scatter.4.cloned.1.call-start = ((), (), s32[]{:S(2)}) async-start(), calls=%async_computation.3 | async-start | bytes 1671168
  173.4 263.3 %copy-start.8 = (f32[128]{0:T(128)}, f32[128]{0:T(128)S(1)}, u32[]{:S(2)}) copy-start(f32[128]{0:T(128)S(1)} %broadcast_multiply_fusion.7) | copy-start | bytes 1540
  175.4 261.3 %copy-start.6 = (f32[128]{0:T(128)}, f32[128]{0:T(128)S(1)}, u32[]{:S(2)}) copy-start(f32[128]{0:T(128)S(1)} %add_rsqrt_fusion.2) | copy-start | bytes 1540
  417.5 19.1 %copy-start.1 = (bf16[128,6144]{1,0:T(8,128)(2,1)S(1)}, bf16[128,6144]{1,0:T(8,128)(2,1)}, u32[]{:S(2)}) copy-start(bf16[128,6144]{1,0:T(8,128)(2,1)} %all-gather.7.cloned.1.call-done) | copy-start | bytes 4718596
  442.0 0.7 copy-start.2
  443.2 0.7 copy-start.3
  472.6 2.6 copy-start.5
  472.6 2.6 copy-start.7
  472.6 2.7 copy-start.9
Sparse Core Ops, SparseCore 0:
  10.5 88.3 all-gather.6
  131.7 285.7 all-gather.4
  475.3 106.3 reduce-scatter.3
where the time goes:
time: 658 us; the launch traced here: 651 us
  waiting for transfers between devices  347 us (53%)
  blocking collectives  219 us (33%)
  local copies, waits for them, and re-layouts  35 us (5%)
  matrix products  20 us (3%)
  other arithmetic  16 us (2%)
  between operations  13.4 us (2%)
    all_gather x1, waiting for transfers between devices, per_device(): gathered = lax.all_gather(shifted, 'dp', axis=1, tiled=True)  242 us
    psum x1, blocking collectives, per_device(): lax.psum((weight_squares, grad_squares), ('dp', 'mp'))  120 us
    unnamed x4, waiting for transfers between devices  105 us
    psum x1, blocking collectives, per_device(): lax.psum((jnp.sum(upstream, axis=-1), jnp.sum(upstream * normed_share, ax...  59.1 us
    all_gather x1, blocking collectives, per_device(): lax.all_gather(norm_gain.reshape(1, -1), 'mp', axis=1, tiled=True)  39.9 us
    unnamed x24, local copies, waits for them, and re-layouts  24.1 us
  transfers between devices with their start and end apart: 3, of which 2 were waited for; matrix products, arithmetic and copies ran while one was open for 1% of the time, Pallas kernels for 0%

commit v1 on v0

v1 whole, which is shorter than its diff:
```python
import jax
import jax.numpy as jnp
from jax import lax
from jax.experimental import pallas as pl
from jax.experimental.pallas import tpu as pltpu
from jax.sharding import PartitionSpec as P

MESH = pl.DeviceIdType.MESH
F32, BF16 = jnp.float32, jnp.bfloat16
HD = 128
NX, NY, ZH, ZL, NC = 4, 4, 2, 8, 2
ascent_radius = 0.15


def mm(a, b):
    return lax.dot_general(a, b, (((1,), (0,)), ((), ())), preferred_element_type=F32)


def mm_nt(a, b):
    return lax.dot_general(a, b, (((1,), (1,)), ((), ())), preferred_element_type=F32)


def mm_tn(a, b):
    return lax.dot_general(a, b, (((0,), (0,)), ((), ())), preferred_element_type=F32)


def row_norm(matrix):
    center = matrix - jnp.mean(matrix, axis=-1, keepdims=True)
    inverse = lax.rsqrt(jnp.mean(center * center, axis=-1, keepdims=True) + 1e-06)
    return center * inverse, inverse


def row_norm_back(upstream, normed, inverse):
    first_mean = jnp.mean(upstream, axis=-1, keepdims=True)
    second_mean = jnp.mean(upstream * normed, axis=-1, keepdims=True)
    return (upstream - first_mean - normed * second_mean) * inverse


def columns_to_rows(first, second):
    lane = lax.broadcasted_iota(jnp.int32, (HD, HD), 1)
    both = jnp.where(lane == 0, first, jnp.where(lane == 1, second, 0.0))
    return both.T[0:8]


def rows_to_columns(first, second):
    sub = lax.broadcasted_iota(jnp.int32, (HD, HD), 0)
    both = jnp.where(sub == 0, first, jnp.where(sub == 1, second, 0.0))
    turned = both.T
    return turned[:, 0:1], turned[:, 1:2]


def kernel(
    tok, gain, w, g, cot, out,
    st_z, st_xc, st_y, rs, fin, nin, normed, invc, xc, wall, pf, pown, psend, precv, dbuf, tbuf, tr, sbuf, sr, ubuf, ur,
    st_s, st_r, xs, xr, cs, n3s, ws, wr, ps, pr, ds_, dr, tcs, tcr, ss, srs, us, urs,
):
    n_mp = NX * ZH * NC
    n_z = ZH * ZL
    width = tok.shape[1]
    band = ZH * NC * width
    n_feat = n_mp * width
    rows = w.shape[1]
    dp = lax.axis_index("dp")
    mp = lax.axis_index("mp")
    y, p = lax.div(dp, ZL), lax.rem(dp, ZL)
    x, c = lax.div(mp, ZH * NC), lax.rem(mp, NC)
    zh = lax.rem(lax.div(mp, NC), ZH)
    z = zh * ZL + p
    xcore = x * NC + c

    def dev(x_, y_, zh_, p_, c_):
        return (y_ * ZL + p_, (x_ * ZH + zh_) * NC + c_)

    def dev_z(k):
        return dev(x, y, lax.div(k, ZL), lax.rem(k, ZL), c)

    def dev_xc(k):
        return dev(lax.div(k, NC), y, zh, p, lax.rem(k, NC))

    def dev_y(k):
        return dev(x, k, zh, p, c)

    def dev_mp(k):
        return (dp, k)

    def remote(src, dst, ssem, rsem, device):
        return pltpu.make_async_remote_copy(
            src_ref=src, dst_ref=dst, send_sem=ssem, recv_sem=rsem, device_id=device, device_id_type=MESH
        )

    def others(n, mine, fn):
        def step(i, carry):
            fn(lax.rem(mine + i, n), i)
            return carry

        lax.fori_loop(1, n, step, 0)

    def share(buf, n, mine, dev_of, ssem, rsem):
        others(n, mine, lambda k, i: remote(buf.at[mine], buf.at[mine], ssem, rsem, dev_of(k)).start())

    def arrived(buf, n, sem):
        part = buf.at[pl.ds(0, n - 1)]
        pltpu.make_async_copy(part, part, sem).wait()

    barrier = pltpu.get_barrier_semaphore()

    def greet(device):
        pl.semaphore_signal(barrier, inc=1, device_id=device, device_id_type=MESH)

    others(n_mp, mp, lambda k, i: greet(dev_mp(k)))
    others(NY, y, lambda k, i: greet(dev_y(k)))

    def greet_z(k, i):
        @pl.when(lax.rem(k, ZL) != p)
        def _():
            greet(dev_z(k))

    others(n_z, z, greet_z)

    @pl.when(x != y)
    def _():
        for k in range(ZH):
            greet(dev(y, x, k, p, c))

    st_z[z] = jnp.zeros((16, HD), F32)
    for m in range(4):
        for base, ref in ((0, w), (8, g)):
            values = ref[m].astype(F32)
            sums = jnp.sum(values * values, axis=0, keepdims=True)
            st_z[z, base + m : base + m + 1] = sums[:, :HD] + sums[:, HD:]
    part = tok[...].astype(F32)
    part_mean = jnp.sum(part, axis=-1, keepdims=True) * (1.0 / width)
    part_square = jnp.sum(jnp.square(part - part_mean), axis=-1, keepdims=True)
    rs[mp] = columns_to_rows(part_mean, part_square)

    pl.semaphore_wait(barrier, (n_mp - 1) + (NY - 1) + (n_z - ZH) + jnp.where(x != y, ZH, 0))

    share(st_z, n_z, z, dev_z, st_s.at[0], st_r.at[0])
    share(rs, n_mp, mp, dev_mp, st_s.at[1], st_r.at[1])
    arrived(st_z, n_z, st_r.at[0])
    st_xc[xcore] = jnp.sum(st_z[...], axis=0)
    share(st_xc, NX * NC, xcore, dev_xc, st_s.at[2], st_r.at[2])

    arrived(rs, n_mp, st_r.at[1])
    means = rs[:, 0:1, :]
    mean = jnp.sum(means, axis=0) * (1.0 / n_mp)
    square = jnp.sum(rs[:, 1:2, :], axis=0) + width * jnp.sum(jnp.square(means - mean[None]), axis=0)
    inverse = lax.rsqrt(square * (1.0 / n_feat) + 1e-06)
    mean_col, inv_col = rows_to_columns(mean, inverse)
    normed[...] = (tok[...].astype(F32) - mean_col) * inv_col
    invc[...] = jnp.broadcast_to(inv_col, (HD, HD))
    nin[...] = (normed[...] * gain[...].astype(F32)).astype(BF16)

    for k in range(ZH):
        here = (x == y) & (zh == k)
        dst = xc.at[0, zh * NC + c, y]
        landed = xr.at[0, zh * NC + c, y]

        @pl.when(here)
        def _():
            pltpu.make_async_copy(nin, dst, landed).start()

        @pl.when(jnp.logical_not(here))
        def _():
            remote(nin, dst, xs.at[k], landed, dev(y, x, k, p, c)).start()

    arrived(st_xc, NX * NC, st_r.at[2])
    st_y[y] = jnp.sum(st_xc[...], axis=0)
    share(st_y, NY, y, dev_y, st_s.at[3], st_r.at[3])
    arrived(st_y, NY, st_r.at[3])
    total = jnp.sum(jnp.sum(st_y[...], axis=0), axis=-1, keepdims=True)
    ratio = ascent_radius * jnp.sqrt(total[0:8]) / (jnp.sqrt(total[8:16]) + 1e-12)
    for m in range(4):
        wall[m, p] = (w[m].astype(F32) + ratio[m : m + 1] * g[m].astype(F32)).astype(BF16)

    def weight_copy(way, m, s):
        return remote(
            wall.at[m, s], wall.at[m, s], ws.at[way, m, s], wr.at[m, s], dev(x, y, zh, p + 1 - 2 * way, c)
        )

    def send_weight(way, m, s):
        @pl.when(p < ZL - 1 if way == 0 else p > 0)
        def _():
            weight_copy(way, m, s).start()

    def send_own(ph):
        m = lax.rem(ph + 3, 4)
        send_weight(0, m, p)
        send_weight(1, m, p)

    send_own(0)

    for j in range(ZH * NC):
        pltpu.make_async_copy(
            cot.at[:, pl.ds(pl.multiple_of(y * band + j * width, HD), width)], xc.at[1, j, y], xr.at[1, j, y]
        ).start()

    def send_cot(k, i):
        for j in range(ZH * NC):
            remote(
                cot.at[:, pl.ds(pl.multiple_of(k * band + j * width, HD), width)],
                xc.at[1, j, y],
                cs.at[i, j],
                xr.at[1, j, y],
                dev_y(k),
            ).start()

    others(NY, y, send_cot)

    def wait_block(ref, sem):
        pltpu.make_async_copy(ref, ref, sem).wait()

    def send_tokens():
        for k in range(ZH):
            j = k * NC + c
            wait_block(xc.at[0, j, x], xr.at[0, j, x])
            others(
                NX * NC,
                xcore,
                lambda q, i: remote(
                    xc.at[0, j, x], xc.at[0, j, x], n3s.at[k, i], xr.at[0, j, x], dev_xc(q)
                ).start(),
            )

    def multiply(ph):
        m = lax.rem(ph + 3, 4)
        sel = jnp.where(ph == 0, 1, 0)

        @pl.when(ph < 2)
        def _():
            def wait_one(i, carry):
                j, tb = lax.div(i, NY), lax.rem(i, NY)

                @pl.when((ph == 0) | (lax.rem(j, NC) != c) | (tb != x))
                def _():
                    wait_block(xc.at[sel, j, tb], xr.at[sel, j, tb])

                return carry

            lax.fori_loop(0, ZH * NC * NY, wait_one, 0)

        columns = wall.shape[3]
        weights = wall[m].reshape(ZL * rows, columns)
        acc = None
        for j in range(ZH * NC):
            left = xc[sel, j].reshape(NY * HD, width)
            term = mm(left, weights[j * width : (j + 1) * width])
            acc = term if acc is None else acc + term
        pf[...] = acc.reshape(NY, HD, columns)
        pown[m] = pf[y]
        psend[m] = pf[...].astype(BF16)
        others(
            NY, y, lambda k, i: remote(psend.at[m, k], precv.at[m, y], ps.at[m, i], pr.at[m, y], dev_y(k)).start()
        )

    def phase(ph, carry):
        @pl.when(ph < 4)
        def _():
            m = lax.rem(ph + 3, 4)

            def hop(t, carry):
                from_low = p - t

                @pl.when(from_low >= 0)
                def _():
                    wait_block(wall.at[m, from_low], wr.at[m, from_low])
                    send_weight(0, m, from_low)

                from_high = p + t

                @pl.when(from_high < ZL)
                def _():
                    wait_block(wall.at[m, from_high], wr.at[m, from_high])
                    send_weight(1, m, from_high)

                @pl.when((t == max(ZL - 3, 1)) & (ph < 3))
                def _():
                    send_own(ph + 1)

                return carry

            lax.fori_loop(1, ZL, hop, 0)

        @pl.when(ph == 0)
        def _():
            send_tokens()

        @pl.when(ph > 0)
        def _():
            multiply(ph - 1)

        return carry

    lax.fori_loop(0, 5, phase, 0)

    def projected(m):
        value = pown[m]
        for i in range(1, NY):
            k = lax.rem(y + i, NY)
            wait_block(precv.at[m, k], pr.at[m, k])
            value = value + precv[m, k].astype(F32)
        return value

    grad_attn_all = projected(3).astype(BF16)
    query_all = projected(0)
    key_all = projected(1)
    value_all = projected(2).astype(BF16)
    score_scale = HD ** (-0.5)
    for h in range(wall.shape[3] // HD):
        cols = slice(h * HD, (h + 1) * HD)
        q_hat, q_inv = row_norm(query_all[:, cols])
        k_hat, k_inv = row_norm(key_all[:, cols])
        queries, key_rows = q_hat.astype(BF16), k_hat.astype(BF16)
        value_rows, grad_attn = value_all[:, cols], grad_attn_all[:, cols]
        exps = jnp.exp(mm_nt(queries, key_rows) * score_scale)
        probs = exps / jnp.sum(exps, axis=-1, keepdims=True)
        grad_values = mm_tn(probs.astype(BF16), grad_attn)
        grad_probs = mm_nt(grad_attn, value_rows)
        inner = jnp.sum(probs * grad_probs, axis=-1, keepdims=True)
        grad_scores = (probs * (grad_probs - inner) * score_scale).astype(BF16)
        grad_query = mm(grad_scores, key_rows)
        grad_keys = mm_tn(grad_scores, queries)
        dbuf[y, 0, :, cols] = row_norm_back(grad_query, q_hat, q_inv).astype(BF16)
        dbuf[y, 1, :, cols] = row_norm_back(grad_keys, k_hat, k_inv).astype(BF16)
        dbuf[y, 2, :, cols] = grad_values.astype(BF16)
    others(NY, y, lambda k, i: remote(dbuf.at[y], dbuf.at[y], ds_.at[i], dr.at[y], dev_y(k)).start())

    def terms(i, carry):
        tb = lax.rem(y + i, NY)

        @pl.when(i > 0)
        def _():
            wait_block(dbuf.at[tb], dr.at[tb])

        for j in range(ZH * NC):
            acc = None
            for m in range(3):
                weights = wall[m].reshape(ZL * rows, wall.shape[3])[j * width : (j + 1) * width]
                term = mm_nt(dbuf[tb, m], weights)
                acc = term if acc is None else acc + term
            tbuf[j % NC, tb, j // NC] = acc.astype(BF16)
        remote(tbuf.at[1 - c, tb], tr.at[tb], tcs.at[tb], tcr.at[tb], dev(x, y, zh, p, 1 - c)).start()
        return carry

    lax.fori_loop(0, NY, terms, 0)

    def add_cores(i, carry):
        tb = lax.rem(y + i, NY)
        wait_block(tr.at[tb], tcr.at[tb])
        sbuf[tb] = (tbuf[c, tb].astype(F32) + tr[tb].astype(F32)).astype(BF16)

        @pl.when(tb != x)
        def _():
            remote(sbuf.at[tb], sr.at[x], ss.at[tb], srs.at[x], dev(tb, y, zh, p, c)).start()

        return carry

    lax.fori_loop(0, NY, add_cores, 0)
    value = sbuf[x].astype(F32)
    for i in range(1, NX):
        k = lax.rem(x + i, NX)
        wait_block(sr.at[k], srs.at[k])
        value = value + sr[k].astype(F32)
    ubuf[...] = value.astype(BF16)
    for k in range(ZH):
        here = (x == y) & (zh == k)

        @pl.when(here)
        def _():
            pltpu.make_async_copy(ubuf.at[k], ur.at[zh], urs.at[zh]).start()

        @pl.when(jnp.logical_not(here))
        def _():
            remote(ubuf.at[k], ur.at[zh], us.at[k], urs.at[zh], dev(y, x, k, p, c)).start()

    for k in range(ZH):
        wait_block(ur.at[k], urs.at[k])
    upstream = (ur[0].astype(F32) + ur[1].astype(F32)) * gain[...].astype(F32)
    fin[mp] = columns_to_rows(
        jnp.sum(upstream, axis=-1, keepdims=True), jnp.sum(upstream * normed[...], axis=-1, keepdims=True)
    )
    share(fin, n_mp, mp, dev_mp, st_s.at[4], st_r.at[4])
    arrived(fin, n_mp, st_r.at[4])
    sums = jnp.sum(fin[...], axis=0) * (1.0 / n_feat)
    first, second = rows_to_columns(sums[0:1], sums[1:2])
    out[...] = ((upstream - first - normed[...] * second) * invc[:, 0:1]).astype(BF16)

    arrived(st_z, n_z, st_s.at[0])
    arrived(rs, n_mp, st_s.at[1])
    arrived(st_xc, NX * NC, st_s.at[2])
    arrived(st_y, NY, st_s.at[3])
    arrived(fin, n_mp, st_s.at[4])
    for k in range(ZH):
        here = (x == y) & (zh == k)

        @pl.when(jnp.logical_not(here))
        def _():
            wait_block(nin, xs.at[k])
            wait_block(ubuf.at[k], us.at[k])

    def left_y(i, carry):
        for j in range(ZH * NC):
            wait_block(xc.at[1, j, 0], cs.at[i, j])
        for m in range(4):
            wait_block(psend.at[m, 0], ps.at[m, i])
        wait_block(dbuf.at[0], ds_.at[i])
        return carry

    lax.fori_loop(1, NY, left_y, 0)

    def left_xc(i, carry):
        for k in range(ZH):
            wait_block(xc.at[0, 0, 0], n3s.at[k, i])
        return carry

    lax.fori_loop(1, NX * NC, left_xc, 0)

    def left_blocks(tb, carry):
        wait_block(tr.at[tb], tcs.at[tb])

        @pl.when(tb != x)
        def _():
            wait_block(sbuf.at[tb], ss.at[tb])

        return carry

    lax.fori_loop(0, NY, left_blocks, 0)

    def left_weights(i, carry):
        m, s = lax.div(i, ZL), lax.rem(i, ZL)

        @pl.when((p < ZL - 1) & (s <= p))
        def _():
            wait_block(wall.at[m, s], ws.at[0, m, s])

        @pl.when((p > 0) & (s >= p))
        def _():
            wait_block(wall.at[m, s], ws.at[1, m, s])

        return carry

    lax.fori_loop(0, 4 * ZL, left_weights, 0)


def per_device(tokens, norm_gain, attn_weights, stored_grads, cotangent):
    width = tokens.shape[1]
    _, rows, columns = attn_weights.shape
    n_mp = NX * ZH * NC
    nj = ZH * NC
    dma = pltpu.SemaphoreType.DMA
    vmem = pl.BlockSpec(memory_space=pltpu.VMEM)
    return pl.pallas_call(
        kernel,
        out_shape=jax.ShapeDtypeStruct((HD, width), BF16),
        in_specs=[vmem, vmem, vmem, vmem, pl.BlockSpec(memory_space=pl.ANY)],
        out_specs=vmem,
        scratch_shapes=[
            pltpu.VMEM((ZH * ZL, 16, HD), F32),
            pltpu.VMEM((NX * NC, 16, HD), F32),
            pltpu.VMEM((NY, 16, HD), F32),
            pltpu.VMEM((n_mp, 8, HD), F32),
            pltpu.VMEM((n_mp, 8, HD), F32),
            pltpu.VMEM((HD, width), BF16),
            pltpu.VMEM((HD, width), F32),
            pltpu.VMEM((HD, HD), F32),
            pltpu.VMEM((2, nj, NY, HD, width), BF16),
            pltpu.VMEM((4, ZL, rows, columns), BF16),
            pltpu.VMEM((NY, HD, columns), F32),
            pltpu.VMEM((4, HD, columns), F32),
            pltpu.VMEM((4, NY, HD, columns), BF16),
            pltpu.VMEM((4, NY, HD, columns), BF16),
            pltpu.VMEM((NY, 3, HD, columns), BF16),
            pltpu.VMEM((NC, NY, ZH, HD, width), BF16),
            pltpu.VMEM((NY, ZH, HD, width), BF16),
            pltpu.VMEM((NY, ZH, HD, width), BF16),
            pltpu.VMEM((NX, ZH, HD, width), BF16),
            pltpu.VMEM((ZH, HD, width), BF16),
            pltpu.VMEM((ZH, HD, width), BF16),
            dma((5,)),
            dma((5,)),
            dma((ZH,)),
            dma((2, nj, NY)),
            dma((NY, nj)),
            dma((ZH, NX * NC)),
            dma((2, 4, ZL)),
            dma((4, ZL)),
            dma((4, NY)),
            dma((4, NY)),
            dma((NY,)),
            dma((NY,)),
            dma((NY,)),
            dma((NY,)),
            dma((NY,)),
            dma((NX,)),
            dma((ZH,)),
            dma((ZH,)),
        ],
        compiler_params=pltpu.CompilerParams(
            collective_id=0, has_side_effects=True, vmem_limit_bytes=48 * 1024 * 1024
        ),
    )(tokens, norm_gain.reshape(1, -1), attn_weights, stored_grads, cotangent)


def solution(mesh):
    return jax.shard_map(
        per_device,
        mesh=mesh,
        in_specs=(P("dp", "mp"), P("mp"), P(None, "dp", "mp"), P(None, "dp", "mp"), P("dp", None)),
        out_specs=P("dp", "mp"),
        check_vma=False,
    )
```

time: 658 us -> 194 us (0.29)
  waiting for transfers between devices: 347 us -> 0 us
  blocking collectives: 219 us -> 0 us
  Pallas kernels: 0 us -> 186 us
  local copies, waits for them, and re-layouts: 35 us -> 5.61 us
  matrix products: 20 us -> 0 us
  other arithmetic: 16 us -> 0 us
  between operations: 13.4 us -> 0.01 us
    all_gather x2 -> x0, waiting for transfers between devices: 242 us -> none  [the longest x1 242 us: per_device(): gathered = lax.all_gather(shifted, 'dp', axis=1, tiled=True)]
    pallas_call x0 -> x1, Pallas kernels: none -> 186 us  [per_device(): pl.pallas_call(kernel, out_shape=jax.ShapeDtypeStruct((HD, width), BF16),...]
    psum x2 -> x0, blocking collectives: 180 us -> none  [the longest x1 120 us: per_device(): lax.psum((weight_squares, grad_squares), ('dp', 'mp'))]
    unnamed x4 -> x0, waiting for transfers between devices: 105 us -> none
    all_gather x1 -> x0, blocking collectives: 39.9 us -> none  [per_device(): lax.all_gather(norm_gain.reshape(1, -1), 'mp', axis=1, tiled=True)]
    dot_general x8 -> x0, matrix products: 20 us -> none  [the longest x1 6.24 us: per_device(): jnp.einsum('mte,mde->td', stacked, project, preferred_element_type=jnp.fl...]
    unnamed x24 -> x9, local copies, waits for them, and re-layouts: 24.1 us -> 4.93 us
    slice x3 -> x0, local copies, waits for them, and re-layouts: 8.65 us -> none  [the longest x1 8.62 us: per_device(): out_proj = gathered[3]]
  transfers between devices with their start and end apart: 3 -> 0, of which waited for: 2 -> 0; matrix products, arithmetic and copies ran while one was open for 1% -> 0% of each run, Pallas kernels for 0% -> 0%
where the time goes in v1:
time: 194 us; the launch traced here: 192 us
  Pallas kernels  186 us (96%)
  local copies, waits for them, and re-layouts  5.61 us (3%)
    pallas_call x1, Pallas kernels, per_device(): pl.pallas_call(kernel, out_shape=jax.ShapeDtypeStruct((HD, width), BF16),...  186 us
    unnamed x9, local copies, waits for them, and re-layouts  4.93 us

profile of v1, /device:TPU:7, one launch (start us, length us, event | category | flops | bytes accessed | tf_op | source)
XLA Modules:
  0.0 192.0 jit_solution(2672310245487861346)
XLA Ops:
  0.0 0.7 reshape.3.gain
  0.7 0.0 copy-start
  0.7 1.4 copy-done
  2.1 0.0 copy-start.1
  2.1 1.0 copy-done.1
  3.1 0.0 copy-start.2
  3.1 1.0 copy-done.2
  4.1 0.0 copy-start.3
  4.1 0.9 copy-done.3
  5.0 186.4 %shard_map.55 = bf16[128,384]{1,0:T(8,128)(2,1)S(1)} custom-call(bf16[128,384]{1,0:T(8,128)(2,1)S(1)} %copy-done.3, bf16[1,384]{1,0:T(2,128)(2,1)S(1)} %reshape.3.gain, bf16[4,192,256]{2,1,0:T(8,128)(2,1)S(1)} %copy-done.1, bf16[4,192,256]{2,1,0:T(8,128)(2,1)S(1)} %copy-done.2, bf16[128,6144]{1,0:T(8,128)(2,1)S(1)} %copy-done), custom_call_target="tpu_custom_call" | custom-call | tf_op jit(solution)/shard_map/pallas_call | solution.py:452
  191.3 0.6 copy.7
Async XLA Ops:
  0.7 1.4 copy-start
  2.1 1.0 copy-start.1
  3.1 1.0 copy-start.2
  4.1 0.9 copy-start.3

commit v2 on v1

v2 whole, which is shorter than its diff:
```python
import jax
import jax.numpy as jnp
from jax import lax
from jax.experimental import pallas as pl
from jax.experimental.pallas import tpu as pltpu
from jax.sharding import PartitionSpec as P

MESH = pl.DeviceIdType.MESH
F32, BF16 = jnp.float32, jnp.bfloat16
HD = 128
NX, NY, ZH, ZL, NC = 4, 4, 2, 8, 2
NH = 2
NR = 2
ascent_radius = 0.15


def mm(a, b):
    return lax.dot_general(a, b, (((1,), (0,)), ((), ())), preferred_element_type=F32)


def mm_nt(a, b):
    return lax.dot_general(a, b, (((1,), (1,)), ((), ())), preferred_element_type=F32)


def mm_tn(a, b):
    return lax.dot_general(a, b, (((0,), (0,)), ((), ())), preferred_element_type=F32)


def row_norm(matrix):
    center = matrix - jnp.mean(matrix, axis=-1, keepdims=True)
    inverse = lax.rsqrt(jnp.mean(center * center, axis=-1, keepdims=True) + 1e-06)
    return center * inverse, inverse


def row_norm_back(upstream, normed, inverse):
    first_mean = jnp.mean(upstream, axis=-1, keepdims=True)
    second_mean = jnp.mean(upstream * normed, axis=-1, keepdims=True)
    return (upstream - first_mean - normed * second_mean) * inverse


def columns_to_rows(first, second):
    lane = lax.broadcasted_iota(jnp.int32, (HD, HD), 1)
    both = jnp.where(lane == 0, first, jnp.where(lane == 1, second, 0.0))
    return both.T[0:8]


def rows_to_columns(first, second):
    sub = lax.broadcasted_iota(jnp.int32, (HD, HD), 0)
    both = jnp.where(sub == 0, first, jnp.where(sub == 1, second, 0.0))
    turned = both.T
    return turned[:, 0:1], turned[:, 1:2]


def kernel(
    tok, gain, w, g, cot, out,
    st_z, st_xyc, rs, gx, fa, fb, nin, normed, invc, xc, wall, pf, pown, psend, precv, dbuf, tbuf, tr, sbuf, sr, ubuf, ur,
    st_s, st_r, gs, gr, fs, xs, xr, cs, n3s, ws, wr, ps, pr, ds_, dr, tcs, tcr, ss, srs, us, urs,
):
    n_mp = NX * ZH * NC
    n_z = ZH * ZL
    width = tok.shape[1]
    band = ZH * NC * width
    n_feat = n_mp * width
    rows = w.shape[1]
    dp = lax.axis_index("dp")
    mp = lax.axis_index("mp")
    y, p = lax.div(dp, ZL), lax.rem(dp, ZL)
    x, c = lax.div(mp, ZH * NC), lax.rem(mp, NC)
    zh = lax.rem(lax.div(mp, NC), ZH)
    z = zh * ZL + p
    xcore = x * NC + c
    xyc = y * NX * NC + xcore
    half = HD // NR
    n_xyc = NX * NY * NC

    def dev(x_, y_, zh_, p_, c_):
        return (y_ * ZL + p_, (x_ * ZH + zh_) * NC + c_)

    def dev_z(k):
        return dev(x, y, lax.div(k, ZL), lax.rem(k, ZL), c)

    def dev_xc(k):
        return dev(lax.div(k, NC), y, zh, p, lax.rem(k, NC))

    def dev_xyc(k):
        return dev(lax.rem(lax.div(k, NC), NX), lax.div(k, NX * NC), zh, p, lax.rem(k, NC))

    def dev_y(k):
        return dev(x, k, zh, p, c)

    def dev_mp(k):
        return (dp, k)

    def remote(src, dst, ssem, rsem, device):
        return pltpu.make_async_remote_copy(
            src_ref=src, dst_ref=dst, send_sem=ssem, recv_sem=rsem, device_id=device, device_id_type=MESH
        )

    def others(n, mine, fn):
        def step(i, carry):
            fn(lax.rem(mine + i, n), i)
            return carry

        lax.fori_loop(1, n, step, 0)

    def share(buf, n, mine, dev_of, ssem, rsem):
        others(n, mine, lambda k, i: remote(buf.at[mine], buf.at[mine], ssem, rsem, dev_of(k)).start())

    def arrived(buf, n, sem):
        part = buf.at[pl.ds(0, n - 1)]
        pltpu.make_async_copy(part, part, sem).wait()

    barrier = pltpu.get_barrier_semaphore()

    def greet(device):
        pl.semaphore_signal(barrier, inc=1, device_id=device, device_id_type=MESH)

    others(n_z, z, lambda k, i: greet(dev_z(k)))
    others(n_xyc, xyc, lambda k, i: greet(dev_xyc(k)))

    def greet_mp(k, i):
        far = lax.rem(lax.div(k, NC), ZH) != zh

        @pl.when(far & ((lax.div(k, ZH * NC) != x) | (lax.rem(k, NC) != c)))
        def _():
            greet(dev_mp(k))

    others(n_mp, mp, greet_mp)

    def greet_turned(k, i):
        @pl.when(x != y)
        def _():
            greet(dev(y, x, k, p, c))

    others(ZH, zh, greet_turned)

    lane = lax.broadcasted_iota(jnp.int32, (1, HD), 1)
    row = jnp.zeros((1, HD), F32)
    for m in range(4):
        for base, ref in ((0, w), (4, g)):
            values = ref[m].astype(F32)
            sums = jnp.sum(values * values, axis=0, keepdims=True)
            row = jnp.where(lane == base + m, jnp.sum(sums, axis=1, keepdims=True), row)
    st_z[z] = row
    part = tok[...].astype(F32)
    part_mean = jnp.sum(part, axis=-1, keepdims=True) * (1.0 / width)
    part_square = jnp.sum(jnp.square(part - part_mean), axis=-1, keepdims=True)
    rs[mp] = columns_to_rows(part_mean, part_square)[0:2]
    gx_row = jnp.broadcast_to(gain[...].astype(F32), (8, width))
    gx[ZH] = gx_row

    pl.semaphore_wait(
        barrier, (n_z - 1) + (n_xyc - 1) + (ZH - 1) * (NX * NC - 1) + jnp.where(x != y, ZH - 1, 0)
    )

    share(st_z, n_z, z, dev_z, st_s.at[0], st_r.at[0])
    share(rs, n_mp, mp, dev_mp, st_s.at[1], st_r.at[1])
    arrived(st_z, n_z, st_r.at[0])
    st_xyc[xyc] = jnp.sum(st_z[...], axis=0)
    share(st_xyc, n_xyc, xyc, dev_xyc, st_s.at[2], st_r.at[2])

    arrived(rs, n_mp, st_r.at[1])
    means = rs[:, 0:1, :]
    mean = jnp.sum(means, axis=0) * (1.0 / n_mp)
    square = jnp.sum(rs[:, 1:2, :], axis=0) + width * jnp.sum(jnp.square(means - mean[None]), axis=0)
    inverse = lax.rsqrt(square * (1.0 / n_feat) + 1e-06)
    mean_col, inv_col = rows_to_columns(mean, inverse)
    normed[...] = (tok[...].astype(F32) - mean_col) * inv_col
    invc[...] = jnp.broadcast_to(inv_col, (HD, HD))
    nin[...] = (normed[...] * gain[...].astype(F32)).astype(BF16)

    for k in range(ZH):
        here = (x == y) & (zh == k)
        dst = xc.at[0, zh * NC + c, y]
        landed = xr.at[0, zh * NC + c, y]

        @pl.when(here)
        def _():
            pltpu.make_async_copy(nin, dst, landed).start()
            pltpu.make_async_copy(gx.at[ZH], gx.at[zh], gr.at[zh]).start()

        @pl.when(jnp.logical_not(here))
        def _():
            remote(nin, dst, xs.at[k], landed, dev(y, x, k, p, c)).start()
            remote(gx.at[ZH], gx.at[zh], gs.at[k], gr.at[zh], dev(y, x, k, p, c)).start()

    arrived(st_xyc, n_xyc, st_r.at[2])
    total = jnp.sum(st_xyc[...], axis=0)
    piece = rows // NH
    for m in range(4):
        ratio = (
            ascent_radius * jnp.sqrt(total[:, m : m + 1]) / (jnp.sqrt(total[:, 4 + m : 5 + m]) + 1e-12)
        )
        shifted = (w[m].astype(F32) + ratio * g[m].astype(F32)).astype(BF16)
        for h in range(NH):
            wall[m, p, h] = shifted[h * piece : (h + 1) * piece]

    def send_weight(way, m, s, h):
        @pl.when(p < ZL - 1 if way == 0 else p > 0)
        def _():
            block = wall.at[m, s, h]
            remote(
                block, block, ws.at[way, m, s, h], wr.at[m, s, h], dev(x, y, zh, p + 1 - 2 * way, c)
            ).start()

    def send_own(ph):
        m = lax.rem(ph + 3, 4)
        for h in range(NH):
            send_weight(0, m, p, h)
            send_weight(1, m, p, h)

    send_own(0)

    for j in range(ZH * NC):
        pltpu.make_async_copy(
            cot.at[:, pl.ds(pl.multiple_of(y * band + j * width, HD), width)], xc.at[1, j, y], xr.at[1, j, y]
        ).start()

    def send_cot(k, i):
        for j in range(ZH * NC):
            remote(
                cot.at[:, pl.ds(pl.multiple_of(k * band + j * width, HD), width)],
                xc.at[1, j, y],
                cs.at[i, j],
                xr.at[1, j, y],
                dev_y(k),
            ).start()

    others(NY, y, send_cot)

    def wait_block(ref, sem):
        pltpu.make_async_copy(ref, ref, sem).wait()

    def send_tokens():
        for k in range(ZH):
            j = k * NC + c
            wait_block(xc.at[0, j, x], xr.at[0, j, x])
            others(
                NX * NC,
                xcore,
                lambda q, i: remote(
                    xc.at[0, j, x], xc.at[0, j, x], n3s.at[k, i], xr.at[0, j, x], dev_xc(q)
                ).start(),
            )

    def multiply(ph):
        m = lax.rem(ph + 3, 4)
        sel = jnp.where(ph == 0, 1, 0)

        @pl.when(ph < 2)
        def _():
            def wait_one(i, carry):
                j, tb = lax.div(i, NY), lax.rem(i, NY)

                @pl.when((ph == 0) | (lax.rem(j, NC) != c) | (tb != x))
                def _():
                    wait_block(xc.at[sel, j, tb], xr.at[sel, j, tb])

                return carry

            lax.fori_loop(0, ZH * NC * NY, wait_one, 0)

        columns = wall.shape[4]
        weights = wall[m].reshape(ZL * rows, columns)
        acc = None
        for j in range(ZH * NC):
            left = xc[sel, j].reshape(NY * HD, width)
            term = mm(left, weights[j * width : (j + 1) * width])
            acc = term if acc is None else acc + term
        pf[...] = acc.reshape(NY, HD, columns)
        pown[m] = pf[y]
        psend[m] = pf[...].astype(BF16)
        others(
            NY, y, lambda k, i: remote(psend.at[m, k], precv.at[m, y], ps.at[m, i], pr.at[m, y], dev_y(k)).start()
        )

    def phase(ph, carry):
        m = lax.rem(ph + 3, 4)

        def hop(t, carry):
            from_low = p - t
            from_high = p + t
            for h in range(NH):

                @pl.when(from_low >= 0)
                def _():
                    wait_block(wall.at[m, from_low, h], wr.at[m, from_low, h])
                    send_weight(0, m, from_low, h)

                @pl.when(from_high < ZL)
                def _():
                    wait_block(wall.at[m, from_high, h], wr.at[m, from_high, h])
                    send_weight(1, m, from_high, h)

            @pl.when((t == max(ZL - 2, 1)) & (ph < 3))
            def _():
                send_own(ph + 1)

            @pl.when((t == min(6, ZL - 1)) & (ph == 0))
            def _():
                send_tokens()

            @pl.when((t == min(4, ZL - 1)) & (ph > 0))
            def _():
                multiply(ph - 1)

            return carry

        lax.fori_loop(1, ZL, hop, 0)
        return carry

    lax.fori_loop(0, 4, phase, 0)
    multiply(3)

    def projected(m):
        value = pown[m]
        for i in range(1, NY):
            k = lax.rem(y + i, NY)
            wait_block(precv.at[m, k], pr.at[m, k])
            value = value + precv[m, k].astype(F32)
        return value

    grad_attn_all = projected(3).astype(BF16)
    query_all = projected(0)
    key_all = projected(1)
    value_all = projected(2).astype(BF16)
    score_scale = HD ** (-0.5)
    for h in range(wall.shape[4] // HD):
        cols = slice(h * HD, (h + 1) * HD)
        q_hat, q_inv = row_norm(query_all[:, cols])
        k_hat, k_inv = row_norm(key_all[:, cols])
        queries, key_rows = q_hat.astype(BF16), k_hat.astype(BF16)
        value_rows, grad_attn = value_all[:, cols], grad_attn_all[:, cols]
        exps = jnp.exp(mm_nt(queries, key_rows) * score_scale)
        probs = exps / jnp.sum(exps, axis=-1, keepdims=True)
        grad_values = mm_tn(probs.astype(BF16), grad_attn)
        grad_probs = mm_nt(grad_attn, value_rows)
        inner = jnp.sum(probs * grad_probs, axis=-1, keepdims=True)
        grad_scores = (probs * (grad_probs - inner) * score_scale).astype(BF16)
        grad_query = mm(grad_scores, key_rows)
        grad_keys = mm_tn(grad_scores, queries)
        grads = (
            row_norm_back(grad_query, q_hat, q_inv).astype(BF16),
            row_norm_back(grad_keys, k_hat, k_inv).astype(BF16),
            grad_values.astype(BF16),
        )
        for m in range(3):
            for r in range(NR):
                dbuf[r, y, m, :, cols] = grads[m][r * half : (r + 1) * half]
    for r in range(NR):
        others(
            NY, y, lambda k, i: remote(dbuf.at[r, y], dbuf.at[r, y], ds_.at[r, i], dr.at[r, y], dev_y(k)).start()
        )

    def term_block(r, tb, own):
        if not own:
            wait_block(dbuf.at[r, tb], dr.at[r, tb])
        for j in range(ZH * NC):
            acc = None
            for m in range(3):
                weights = wall[m].reshape(ZL * rows, wall.shape[4])[j * width : (j + 1) * width]
                term = mm_nt(dbuf[r, tb, m], weights)
                acc = term if acc is None else acc + term
            tbuf[j % NC, r, tb, j // NC] = acc.astype(BF16)
        remote(
            tbuf.at[1 - c, r, tb], tr.at[r, tb], tcs.at[r, tb], tcr.at[r, tb], dev(x, y, zh, p, 1 - c)
        ).start()

    def add_cores(r, tb):
        wait_block(tr.at[r, tb], tcr.at[r, tb])
        sbuf[r, tb] = (tbuf[c, r, tb].astype(F32) + tr[r, tb].astype(F32)).astype(BF16)

        @pl.when(tb != x)
        def _():
            remote(sbuf.at[r, tb], sr.at[r, x], ss.at[r, tb], srs.at[r, x], dev(tb, y, zh, p, c)).start()

    order = [0, 1, 3, 2] if NY == 4 else list(range(NY))
    for r in range(NR):
        before = None
        for i in order:
            tb = lax.rem(y + i, NY)
            term_block(r, tb, i == 0)
            if before is not None:
                add_cores(r, before)
            before = tb
        add_cores(r, before)

    for k in range(ZH):
        wait_block(gx.at[k], gr.at[k])
    firsts, seconds = [], []
    for r in range(NR):
        value = sbuf[r, x].astype(F32)
        for i in range(1, NX):
            k = lax.rem(x + i, NX)
            wait_block(sr.at[r, k], srs.at[r, k])
            value = value + sr[r, k].astype(F32)
        ubuf[r] = value.astype(BF16)
        for k in range(ZH):
            here = (x == y) & (zh == k)

            @pl.when(here)
            def _():
                pltpu.make_async_copy(ubuf.at[r, k], ur.at[r, zh], urs.at[r, zh]).start()

            @pl.when(jnp.logical_not(here))
            def _():
                remote(ubuf.at[r, k], ur.at[r, zh], us.at[r, k], urs.at[r, zh], dev(y, x, k, p, c)).start()

        first, second = 0.0, 0.0
        for k in range(ZH):
            tokens_in = xc[0, k * NC + c, x, r * half : (r + 1) * half].astype(F32)
            first = first + jnp.sum(value[k] * gx[k, 0:1], axis=-1, keepdims=True)
            second = second + jnp.sum(value[k] * tokens_in, axis=-1, keepdims=True)
        firsts.append(first)
        seconds.append(second)
    fa[zh] = columns_to_rows(jnp.concatenate(firsts, axis=0), jnp.concatenate(seconds, axis=0))[0:2]
    share(fa, ZH, zh, lambda k: dev(x, y, k, p, c), st_s.at[3], st_r.at[3])
    arrived(fa, ZH, st_r.at[3])
    fb[NY * NC] = jnp.sum(fa[...], axis=0)
    yc = y * NC + c

    def send_sums(i, carry):
        device = dev(lax.div(i, NC), x, zh, p, lax.rem(i, NC))
        here = (x == y) & (i == xcore)

        @pl.when(here)
        def _():
            pltpu.make_async_copy(fb.at[NY * NC], fb.at[yc], st_r.at[4]).start()

        @pl.when(jnp.logical_not(here))
        def _():
            remote(fb.at[NY * NC], fb.at[yc], fs.at[i], st_r.at[4], device).start()

        return carry

    lax.fori_loop(0, NX * NC, send_sums, 0)
    for r in range(NR):
        for k in range(ZH):
            wait_block(ur.at[r, k], urs.at[r, k])
    arrived(fb, NY * NC + 1, st_r.at[4])
    sums = jnp.sum(fb[0 : NY * NC], axis=0) * (1.0 / n_feat)
    first, second = rows_to_columns(sums[0:1], sums[1:2])
    for r in range(NR):
        part = slice(r * half, (r + 1) * half)
        share_sum = ur[r, 0].astype(F32)
        for k in range(1, ZH):
            share_sum = share_sum + ur[r, k].astype(F32)
        upstream = share_sum * gain[...].astype(F32)
        out[part] = ((upstream - first[part] - normed[part] * second[part]) * invc[part, 0:1]).astype(BF16)

    arrived(st_z, n_z, st_s.at[0])
    arrived(rs, n_mp, st_s.at[1])
    arrived(st_xyc, n_xyc, st_s.at[2])
    arrived(fa, ZH, st_s.at[3])
    for k in range(ZH):
        here = (x == y) & (zh == k)

        @pl.when(jnp.logical_not(here))
        def _():
            wait_block(nin, xs.at[k])
            wait_block(gx.at[ZH], gs.at[k])
            for r in range(NR):
                wait_block(ubuf.at[r, k], us.at[r, k])

    def left_y(i, carry):
        for j in range(ZH * NC):
            wait_block(xc.at[1, j, 0], cs.at[i, j])
        for m in range(4):
            wait_block(psend.at[m, 0], ps.at[m, i])
        for r in range(NR):
            wait_block(dbuf.at[r, 0], ds_.at[r, i])
        return carry

    lax.fori_loop(1, NY, left_y, 0)

    def left_xc(i, carry):
        @pl.when(i > 0)
        def _():
            for k in range(ZH):
                wait_block(xc.at[0, 0, 0], n3s.at[k, i])

        @pl.when((x != y) | (i != xcore))
        def _():
            wait_block(fb.at[0], fs.at[i])

        return carry

    lax.fori_loop(0, NX * NC, left_xc, 0)

    def left_blocks(tb, carry):
        for r in range(NR):
            wait_block(tr.at[r, tb], tcs.at[r, tb])

        @pl.when(tb != x)
        def _():
            for r in range(NR):
                wait_block(sbuf.at[r, tb], ss.at[r, tb])

        return carry

    lax.fori_loop(0, NY, left_blocks, 0)

    def left_weights(i, carry):
        m, s = lax.div(i, ZL), lax.rem(i, ZL)
        for h in range(NH):

            @pl.when((p < ZL - 1) & (s <= p))
            def _():
                wait_block(wall.at[m, s, h], ws.at[0, m, s, h])

            @pl.when((p > 0) & (s >= p))
            def _():
                wait_block(wall.at[m, s, h], ws.at[1, m, s, h])

        return carry

    lax.fori_loop(0, 4 * ZL, left_weights, 0)


def per_device(tokens, norm_gain, attn_weights, stored_grads, cotangent):
    width = tokens.shape[1]
    _, rows, columns = attn_weights.shape
    n_mp = NX * ZH * NC
    nj = ZH * NC
    dma = pltpu.SemaphoreType.DMA
    vmem = pl.BlockSpec(memory_space=pltpu.VMEM)
    return pl.pallas_call(
        kernel,
        out_shape=jax.ShapeDtypeStruct((HD, width), BF16),
        in_specs=[vmem, vmem, vmem, vmem, pl.BlockSpec(memory_space=pl.ANY)],
        out_specs=vmem,
        scratch_shapes=[
            pltpu.VMEM((ZH * ZL, 1, HD), F32),
            pltpu.VMEM((NX * NY * NC, 1, HD), F32),
            pltpu.VMEM((n_mp, 2, HD), F32),
            pltpu.VMEM((ZH + 1, 8, width), F32),
            pltpu.VMEM((ZH, 2, HD), F32),
            pltpu.VMEM((NY * NC + 1, 2, HD), F32),
            pltpu.VMEM((HD, width), BF16),
            pltpu.VMEM((HD, width), F32),
            pltpu.VMEM((HD, HD), F32),
            pltpu.VMEM((2, nj, NY, HD, width), BF16),
            pltpu.VMEM((4, ZL, NH, rows // NH, columns), BF16),
            pltpu.VMEM((NY, HD, columns), F32),
            pltpu.VMEM((4, HD, columns), F32),
            pltpu.VMEM((4, NY, HD, columns), BF16),
            pltpu.VMEM((4, NY, HD, columns), BF16),
            pltpu.VMEM((NR, NY, 3, HD // NR, columns), BF16),
            pltpu.VMEM((NC, NR, NY, ZH, HD // NR, width), BF16),
            pltpu.VMEM((NR, NY, ZH, HD // NR, width), BF16),
            pltpu.VMEM((NR, NY, ZH, HD // NR, width), BF16),
            pltpu.VMEM((NR, NX, ZH, HD // NR, width), BF16),
            pltpu.VMEM((NR, ZH, HD // NR, width), BF16),
            pltpu.VMEM((NR, ZH, HD // NR, width), BF16),
            dma((4,)),
            dma((5,)),
            dma((ZH,)),
            dma((ZH,)),
            dma((NX * NC,)),
            dma((ZH,)),
            dma((2, nj, NY)),
            dma((NY, nj)),
            dma((ZH, NX * NC)),
            dma((2, 4, ZL, NH)),
            dma((4, ZL, NH)),
            dma((4, NY)),
            dma((4, NY)),
            dma((NR, NY)),
            dma((NR, NY)),
            dma((NR, NY)),
            dma((NR, NY)),
            dma((NR, NY)),
            dma((NR, NX)),
            dma((NR, ZH)),
            dma((NR, ZH)),
        ],
        compiler_params=pltpu.CompilerParams(
            collective_id=0, has_side_effects=True, vmem_limit_bytes=48 * 1024 * 1024
        ),
    )(tokens, norm_gain.reshape(1, -1), attn_weights, stored_grads, cotangent)


def solution(mesh):
    return jax.shard_map(
        per_device,
        mesh=mesh,
        in_specs=(P("dp", "mp"), P("mp"), P(None, "dp", "mp"), P(None, "dp", "mp"), P("dp", None)),
        out_specs=P("dp", "mp"),
        check_vma=False,
    )
```

time: 194 us -> 175 us (0.902)
  Pallas kernels: 186 us -> 168 us
    pallas_call x1, Pallas kernels: 186 us -> 168 us  [per_device(): pl.pallas_call(kernel, out_shape=jax.ShapeDtypeStruct((HD, width), BF16),...]
where the time goes in v2:
time: 175 us; the launch traced here: 174 us
  Pallas kernels  168 us (96%)
  local copies, waits for them, and re-layouts  5.61 us (3%)
    pallas_call x1, Pallas kernels, per_device(): pl.pallas_call(kernel, out_shape=jax.ShapeDtypeStruct((HD, width), BF16),...  168 us
    unnamed x9, local copies, waits for them, and re-layouts  4.93 us

profile of v2, /device:TPU:7, one launch (start us, length us, event | category | flops | bytes accessed | tf_op | source)
XLA Modules:
  0.0 174.1 jit_solution(6856573501549195762)
XLA Ops:
  0.0 0.7 reshape.3.gain
  0.7 0.0 copy-start
  0.7 1.4 copy-done
  2.1 0.0 copy-start.1
  2.1 1.0 copy-done.1
  3.1 0.0 copy-start.2
  3.1 1.0 copy-done.2
  4.1 0.0 copy-start.3
  4.1 0.9 copy-done.3
  5.0 168.4 %shard_map.55 = bf16[128,384]{1,0:T(8,128)(2,1)S(1)} custom-call(bf16[128,384]{1,0:T(8,128)(2,1)S(1)} %copy-done.3, bf16[1,384]{1,0:T(2,128)(2,1)S(1)} %reshape.3.gain, bf16[4,192,256]{2,1,0:T(8,128)(2,1)S(1)} %copy-done.1, bf16[4,192,256]{2,1,0:T(8,128)(2,1)S(1)} %copy-done.2, bf16[128,6144]{1,0:T(8,128)(2,1)S(1)} %copy-done), custom_call_target="tpu_custom_call" | custom-call | tf_op jit(solution)/shard_map/pallas_call | solution.py:527
  173.4 0.6 copy.7
Async XLA Ops:
  0.7 1.4 copy-start
  2.1 1.0 copy-start.1
  3.1 1.0 copy-start.2
  4.1 0.9 copy-start.3

commit v3 on v2

--- a/solution.py
+++ b/solution.py
@@ -52,9 +52,10 @@
 
 
 def kernel(
-    tok, gain, w, g, cot, out,
+    tok_hbm, gain_hbm, w_hbm, g_hbm, cot, out,
+    tok, gain, w, g,
     st_z, st_xyc, rs, gx, fa, fb, nin, normed, invc, xc, wall, pf, pown, psend, precv, dbuf, tbuf, tr, sbuf, sr, ubuf, ur,
-    st_s, st_r, gs, gr, fs, xs, xr, cs, n3s, ws, wr, ps, pr, ds_, dr, tcs, tcr, ss, srs, us, urs,
+    ins, st_s, st_r, gs, gr, fs, xs, xr, cs, n3s, ws, wr, ps, pr, ds_, dr, tcs, tcr, ss, srs, us, urs,
 ):
     n_mp = NX * ZH * NC
     n_z = ZH * ZL
@@ -79,61 +80,60 @@
     def dev_z(k):
         return dev(x, y, lax.div(k, ZL), lax.rem(k, ZL), c)
 
-    def dev_xc(k):
-        return dev(lax.div(k, NC), y, zh, p, lax.rem(k, NC))
-
-    def dev_xyc(k):
-        return dev(lax.rem(lax.div(k, NC), NX), lax.div(k, NX * NC), zh, p, lax.rem(k, NC))
-
     def dev_y(k):
         return dev(x, k, zh, p, c)
-
-    def dev_mp(k):
-        return (dp, k)
 
     def remote(src, dst, ssem, rsem, device):
         return pltpu.make_async_remote_copy(
             src_ref=src, dst_ref=dst, send_sem=ssem, recv_sem=rsem, device_id=device, device_id_type=MESH
         )
 
-    def others(n, mine, fn):
-        def step(i, carry):
-            fn(lax.rem(mine + i, n), i)
-            return carry
-
-        lax.fori_loop(1, n, step, 0)
-
-    def share(buf, n, mine, dev_of, ssem, rsem):
-        others(n, mine, lambda k, i: remote(buf.at[mine], buf.at[mine], ssem, rsem, dev_of(k)).start())
+    def share(buf, mine, peers, ssem, rsem):
+        for device in peers:
+            remote(buf.at[mine], buf.at[mine], ssem, rsem, device).start()
 
     def arrived(buf, n, sem):
         part = buf.at[pl.ds(0, n - 1)]
         pltpu.make_async_copy(part, part, sem).wait()
 
+    loads = [
+        pltpu.make_async_copy(src, dst, ins.at[i])
+        for i, (src, dst) in enumerate(((w_hbm, w), (g_hbm, g), (tok_hbm, tok), (gain_hbm, gain)))
+    ]
+    for load in loads:
+        load.start()
+
     barrier = pltpu.get_barrier_semaphore()
 
     def greet(device):
         pl.semaphore_signal(barrier, inc=1, device_id=device, device_id_type=MESH)
 
-    others(n_z, z, lambda k, i: greet(dev_z(k)))
-    others(n_xyc, xyc, lambda k, i: greet(dev_xyc(k)))
-
-    def greet_mp(k, i):
-        far = lax.rem(lax.div(k, NC), ZH) != zh
-
-        @pl.when(far & ((lax.div(k, ZH * NC) != x) | (lax.rem(k, NC) != c)))
-        def _():
-            greet(dev_mp(k))
-
-    others(n_mp, mp, greet_mp)
-
-    def greet_turned(k, i):
-        @pl.when(x != y)
-        def _():
-            greet(dev(y, x, k, p, c))
-
-    others(ZH, zh, greet_turned)
-
+    z_peers = []
+    for i in range(1, n_z):
+        k = lax.rem(z + i, n_z)
+        z_peers.append((k, dev_z(k)))
+    at_x = [lax.rem(x + i, NX) for i in range(NX)]
+    at_y = [lax.rem(y + i, NY) for i in range(NY)]
+    at_c = [c, 1 - c]
+    at_z = [zh, 1 - zh]
+    plane_peers = [
+        dev(at_x[i], at_y[j], zh, p, at_c[q]) for j in range(NY) for i in range(NX) for q in range(NC) if i + j + q
+    ]
+    near_peers = [dev(at_x[i], y, zh, p, at_c[q]) for i in range(NX) for q in range(NC) if i + q]
+    far_peers = [dev(at_x[i], y, 1 - zh, p, at_c[q]) for i in range(NX) for q in range(NC) if i + q]
+    partner = dev(x, y, 1 - zh, p, c)
+    y_peers = [(at_y[i], dev_y(at_y[i])) for i in range(1, NY)]
+    for _, device in z_peers:
+        greet(device)
+    for device in far_peers + plane_peers:
+        greet(device)
+
+    @pl.when(x != y)
+    def _():
+        greet(dev(y, x, 1 - zh, p, c))
+
+    loads[0].wait()
+    loads[1].wait()
     lane = lax.broadcasted_iota(jnp.int32, (1, HD), 1)
     row = jnp.zeros((1, HD), F32)
     for m in range(4):
@@ -142,22 +142,24 @@
             sums = jnp.sum(values * values, axis=0, keepdims=True)
             row = jnp.where(lane == base + m, jnp.sum(sums, axis=1, keepdims=True), row)
     st_z[z] = row
+    loads[2].wait()
+    loads[3].wait()
     part = tok[...].astype(F32)
     part_mean = jnp.sum(part, axis=-1, keepdims=True) * (1.0 / width)
     part_square = jnp.sum(jnp.square(part - part_mean), axis=-1, keepdims=True)
     rs[mp] = columns_to_rows(part_mean, part_square)[0:2]
-    gx_row = jnp.broadcast_to(gain[...].astype(F32), (8, width))
+    gx_row = jnp.broadcast_to(gain[...].astype(F32).reshape(1, -1), (8, width))
     gx[ZH] = gx_row
 
     pl.semaphore_wait(
         barrier, (n_z - 1) + (n_xyc - 1) + (ZH - 1) * (NX * NC - 1) + jnp.where(x != y, ZH - 1, 0)
     )
 
-    share(st_z, n_z, z, dev_z, st_s.at[0], st_r.at[0])
-    share(rs, n_mp, mp, dev_mp, st_s.at[1], st_r.at[1])
+    share(st_z, z, [d for _, d in z_peers], st_s.at[0], st_r.at[0])
+    share(rs, mp, near_peers + [partner] + far_peers, st_s.at[1], st_r.at[1])
     arrived(st_z, n_z, st_r.at[0])
     st_xyc[xyc] = jnp.sum(st_z[...], axis=0)
-    share(st_xyc, n_xyc, xyc, dev_xyc, st_s.at[2], st_r.at[2])
+    share(st_xyc, xyc, plane_peers, st_s.at[2], st_r.at[2])
 
     arrived(rs, n_mp, st_r.at[1])
     means = rs[:, 0:1, :]
@@ -167,7 +169,7 @@
     mean_col, inv_col = rows_to_columns(mean, inverse)
     normed[...] = (tok[...].astype(F32) - mean_col) * inv_col
     invc[...] = jnp.broadcast_to(inv_col, (HD, HD))
-    nin[...] = (normed[...] * gain[...].astype(F32)).astype(BF16)
+    nin[...] = (normed[...] * gain[...].astype(F32).reshape(1, -1)).astype(BF16)
 
     for k in range(ZH):
         here = (x == y) & (zh == k)
@@ -195,6 +197,8 @@
         for h in range(NH):
             wall[m, p, h] = shifted[h * piece : (h + 1) * piece]
 
+    pairs = ((3, 0), (1, 2))
+
     def send_weight(way, m, s, h):
         @pl.when(p < ZL - 1 if way == 0 else p > 0)
         def _():
@@ -204,10 +208,10 @@
             ).start()
 
     def send_own(ph):
-        m = lax.rem(ph + 3, 4)
-        for h in range(NH):
-            send_weight(0, m, p, h)
-            send_weight(1, m, p, h)
+        for m in pairs[ph]:
+            for h in range(NH):
+                send_weight(0, m, p, h)
+                send_weight(1, m, p, h)
 
     send_own(0)
 
@@ -216,17 +220,15 @@
             cot.at[:, pl.ds(pl.multiple_of(y * band + j * width, HD), width)], xc.at[1, j, y], xr.at[1, j, y]
         ).start()
 
-    def send_cot(k, i):
+    for i, (k, device) in enumerate(y_peers):
         for j in range(ZH * NC):
             remote(
                 cot.at[:, pl.ds(pl.multiple_of(k * band + j * width, HD), width)],
                 xc.at[1, j, y],
                 cs.at[i, j],
                 xr.at[1, j, y],
-                dev_y(k),
+                device,
             ).start()
-
-    others(NY, y, send_cot)
 
     def wait_block(ref, sem):
         pltpu.make_async_copy(ref, ref, sem).wait()
@@ -234,25 +236,18 @@
     def send_tokens():
         for k in range(ZH):
             j = k * NC + c
-            wait_block(xc.at[0, j, x], xr.at[0, j, x])
-            others(
-                NX * NC,
-                xcore,
-                lambda q, i: remote(
-                    xc.at[0, j, x], xc.at[0, j, x], n3s.at[k, i], xr.at[0, j, x], dev_xc(q)
-                ).start(),
-            )
-
-    def multiply(ph):
-        m = lax.rem(ph + 3, 4)
-        sel = jnp.where(ph == 0, 1, 0)
-
-        @pl.when(ph < 2)
-        def _():
+            block = xc.at[0, j, x]
+            wait_block(block, xr.at[0, j, x])
+            for i, device in enumerate(near_peers):
+                remote(block, block, n3s.at[k, i], xr.at[0, j, x], device).start()
+
+    def multiply(m, sel, fresh):
+        if fresh:
+
             def wait_one(i, carry):
                 j, tb = lax.div(i, NY), lax.rem(i, NY)
 
-                @pl.when((ph == 0) | (lax.rem(j, NC) != c) | (tb != x))
+                @pl.when((sel == 1) | (lax.rem(j, NC) != c) | (tb != x))
                 def _():
                     wait_block(xc.at[sel, j, tb], xr.at[sel, j, tb])
 
@@ -270,47 +265,45 @@
         pf[...] = acc.reshape(NY, HD, columns)
         pown[m] = pf[y]
         psend[m] = pf[...].astype(BF16)
-        others(
-            NY, y, lambda k, i: remote(psend.at[m, k], precv.at[m, y], ps.at[m, i], pr.at[m, y], dev_y(k)).start()
-        )
-
-    def phase(ph, carry):
-        m = lax.rem(ph + 3, 4)
-
+        for i, (k, device) in enumerate(y_peers):
+            remote(psend.at[m, k], precv.at[m, y], ps.at[m, i], pr.at[m, y], device).start()
+
+    def phase(ph, middle):
         def hop(t, carry):
             from_low = p - t
             from_high = p + t
-            for h in range(NH):
-
-                @pl.when(from_low >= 0)
-                def _():
-                    wait_block(wall.at[m, from_low, h], wr.at[m, from_low, h])
-                    send_weight(0, m, from_low, h)
-
-                @pl.when(from_high < ZL)
-                def _():
-                    wait_block(wall.at[m, from_high, h], wr.at[m, from_high, h])
-                    send_weight(1, m, from_high, h)
-
-            @pl.when((t == max(ZL - 2, 1)) & (ph < 3))
-            def _():
-                send_own(ph + 1)
-
-            @pl.when((t == min(6, ZL - 1)) & (ph == 0))
-            def _():
-                send_tokens()
-
-            @pl.when((t == min(4, ZL - 1)) & (ph > 0))
-            def _():
-                multiply(ph - 1)
+            for m in pairs[ph]:
+                for h in range(NH):
+
+                    @pl.when(from_low >= 0)
+                    def _():
+                        wait_block(wall.at[m, from_low, h], wr.at[m, from_low, h])
+                        send_weight(0, m, from_low, h)
+
+                    @pl.when(from_high < ZL)
+                    def _():
+                        wait_block(wall.at[m, from_high, h], wr.at[m, from_high, h])
+                        send_weight(1, m, from_high, h)
 
             return carry
 
-        lax.fori_loop(1, ZL, hop, 0)
-        return carry
-
-    lax.fori_loop(0, 4, phase, 0)
-    multiply(3)
+        cut = max(ZL - 2, 2)
+        lax.fori_loop(1, cut, hop, 0)
+        middle()
+        lax.fori_loop(cut, ZL, hop, 0)
+
+    def middle_first():
+        send_own(1)
+        send_tokens()
+
+    def middle_second():
+        multiply(3, 1, True)
+        multiply(0, 0, True)
+
+    phase(0, middle_first)
+    phase(1, middle_second)
+    multiply(1, 0, False)
+    multiply(2, 0, False)
 
     def projected(m):
         value = pown[m]
@@ -348,9 +341,8 @@
             for r in range(NR):
                 dbuf[r, y, m, :, cols] = grads[m][r * half : (r + 1) * half]
     for r in range(NR):
-        others(
-            NY, y, lambda k, i: remote(dbuf.at[r, y], dbuf.at[r, y], ds_.at[r, i], dr.at[r, y], dev_y(k)).start()
-        )
+        for i, (_, device) in enumerate(y_peers):
+            remote(dbuf.at[r, y], dbuf.at[r, y], ds_.at[r, i], dr.at[r, y], device).start()
 
     def term_block(r, tb, own):
         if not own:
@@ -414,7 +406,7 @@
         firsts.append(first)
         seconds.append(second)
     fa[zh] = columns_to_rows(jnp.concatenate(firsts, axis=0), jnp.concatenate(seconds, axis=0))[0:2]
-    share(fa, ZH, zh, lambda k: dev(x, y, k, p, c), st_s.at[3], st_r.at[3])
+    share(fa, zh, [partner], st_s.at[3], st_r.at[3])
     arrived(fa, ZH, st_r.at[3])
     fb[NY * NC] = jnp.sum(fa[...], axis=0)
     yc = y * NC + c
@@ -445,7 +437,7 @@
         share_sum = ur[r, 0].astype(F32)
         for k in range(1, ZH):
             share_sum = share_sum + ur[r, k].astype(F32)
-        upstream = share_sum * gain[...].astype(F32)
+        upstream = share_sum * gain[...].astype(F32).reshape(1, -1)
         out[part] = ((upstream - first[part] - normed[part] * second[part]) * invc[part, 0:1]).astype(BF16)
 
     arrived(st_z, n_z, st_s.at[0])
@@ -471,13 +463,13 @@
             wait_block(dbuf.at[r, 0], ds_.at[r, i])
         return carry
 
-    lax.fori_loop(1, NY, left_y, 0)
+    lax.fori_loop(0, NY - 1, left_y, 0)
 
     def left_xc(i, carry):
         @pl.when(i > 0)
         def _():
             for k in range(ZH):
-                wait_block(xc.at[0, 0, 0], n3s.at[k, i])
+                wait_block(xc.at[0, 0, 0], n3s.at[k, i - 1])
 
         @pl.when((x != y) | (i != xcore))
         def _():
@@ -527,9 +519,13 @@
     return pl.pallas_call(
         kernel,
         out_shape=jax.ShapeDtypeStruct((HD, width), BF16),
-        in_specs=[vmem, vmem, vmem, vmem, pl.BlockSpec(memory_space=pl.ANY)],
+        in_specs=[pl.BlockSpec(memory_space=pltpu.HBM)] * 5,
         out_specs=vmem,
         scratch_shapes=[
+            pltpu.VMEM(tokens.shape, BF16),
+            pltpu.VMEM((width,), BF16),
+            pltpu.VMEM(attn_weights.shape, BF16),
+            pltpu.VMEM(attn_weights.shape, BF16),
             pltpu.VMEM((ZH * ZL, 1, HD), F32),
             pltpu.VMEM((NX * NY * NC, 1, HD), F32),
             pltpu.VMEM((n_mp, 2, HD), F32),
@@ -553,6 +549,7 @@
             pltpu.VMEM((NR, ZH, HD // NR, width), BF16),
             pltpu.VMEM((NR, ZH, HD // NR, width), BF16),
             dma((4,)),
+            dma((4,)),
             dma((5,)),
             dma((ZH,)),
             dma((ZH,)),
@@ -575,9 +572,9 @@
             dma((NR, ZH)),
         ],
         compiler_params=pltpu.CompilerParams(
-            collective_id=0, has_side_effects=True, vmem_limit_bytes=48 * 1024 * 1024
+            collective_id=0, has_side_effects=True, vmem_limit_bytes=60 * 1024 * 1024
         ),
-    )(tokens, norm_gain.reshape(1, -1), attn_weights, stored_grads, cotangent)
+    )(tokens, norm_gain, attn_weights, stored_grads, cotangent)
 
 
 def solution(mesh):

time: 175 us -> 148 us (0.85)
  Pallas kernels: 168 us -> 146 us
  local copies, waits for them, and re-layouts: 5.61 us -> 1.54 us
    pallas_call x1, Pallas kernels: 168 us -> 146 us  [per_device(): pl.pallas_call(kernel, out_shape=jax.ShapeDtypeStruct((HD, width), BF16),...]
    unnamed x9 -> x1, local copies, waits for them, and re-layouts: 4.93 us -> 1.54 us
where the time goes in v3:
time: 148 us; the launch traced here: 147 us
  Pallas kernels  146 us (99%)
  local copies, waits for them, and re-layouts  1.54 us (1%)
    pallas_call x1, Pallas kernels, per_device(): pl.pallas_call(kernel, out_shape=jax.ShapeDtypeStruct((HD, width), BF16),...  146 us

profile of v3, /device:TPU:7, one launch (start us, length us, event | category | flops | bytes accessed | tf_op | source)
XLA Modules:
  0.0 147.1 jit_solution(9817386685107252271)
XLA Ops:
  0.0 145.6 %shard_map.55 = bf16[128,384]{1,0:T(8,128)(2,1)} custom-call(bf16[128,384]{1,0:T(8,128)(2,1)} %tok_hbm.1, bf16[384]{0:T(512)(128)(2,1)} %gain_hbm.1, bf16[4,192,256]{2,1,0:T(8,128)(2,1)} %w_hbm.1, bf16[4,192,256]{2,1,0:T(8,128)(2,1)} %g_hbm.1, bf16[128,6144]{1,0:T(8,128)(2,1)} %cot.1), custom_call_target="tpu_custom_call" | custom-call | tf_op jit(solution)/shard_map/pallas_call | solution.py:519
  145.6 1.5 %copy.7 = bf16[128,384]{1,0:T(8,128)(2,1)} copy(bf16[128,384]{1,0:T(8,128)(2,1)} %shard_map.55) | data formatting | bytes 196608

commit v4 on v3

--- a/solution.py
+++ b/solution.py
@@ -54,8 +54,8 @@
 def kernel(
     tok_hbm, gain_hbm, w_hbm, g_hbm, cot, out,
     tok, gain, w, g,
-    st_z, st_xyc, rs, gx, fa, fb, nin, normed, invc, xc, wall, pf, pown, psend, precv, dbuf, tbuf, tr, sbuf, sr, ubuf, ur,
-    ins, st_s, st_r, gs, gr, fs, xs, xr, cs, n3s, ws, wr, ps, pr, ds_, dr, tcs, tcr, ss, srs, us, urs,
+    st_z, st_xyc, rs, gx, fb, mi, xraw, normed, invc, xc, wall, pf, pown, psend, precv, dbuf, tbuf, tr, sbuf, sr, ubuf, ur,
+    ins, st_s, st_r, gs, gr, fs, ms, xs, xw, xr, cs, n3s, ws, wr, ps, pr, ds_, dr, tcs, tcr, ss, srs, us, urs,
 ):
     n_mp = NX * ZH * NC
     n_z = ZH * ZL
@@ -127,10 +127,13 @@
         greet(device)
     for device in far_peers + plane_peers:
         greet(device)
-
-    @pl.when(x != y)
-    def _():
-        greet(dev(y, x, 1 - zh, p, c))
+    for j in range(1, NY):
+        for i in range(NX):
+
+            @pl.when((at_y[j] == x) | (at_x[i] == y))
+            def _():
+                for q in range(NC):
+                    greet(dev(at_x[i], at_y[j], 1 - zh, p, at_c[q]))
 
     loads[0].wait()
     loads[1].wait()
@@ -151,12 +154,24 @@
     gx_row = jnp.broadcast_to(gain[...].astype(F32).reshape(1, -1), (8, width))
     gx[ZH] = gx_row
 
-    pl.semaphore_wait(
-        barrier, (n_z - 1) + (n_xyc - 1) + (ZH - 1) * (NX * NC - 1) + jnp.where(x != y, ZH - 1, 0)
-    )
+    far_places = jnp.where(x == y, 2 * NX - 1, 3 * NX - 2)
+    pl.semaphore_wait(barrier, (n_z - 1) + (n_xyc - 1) + NC * far_places - 1)
 
     share(st_z, z, [d for _, d in z_peers], st_s.at[0], st_r.at[0])
     share(rs, mp, near_peers + [partner] + far_peers, st_s.at[1], st_r.at[1])
+    for k in at_z[::-1]:
+        here = (x == y) & (zh == k)
+
+        @pl.when(here)
+        def _():
+            pltpu.make_async_copy(tok, xraw.at[zh], xw.at[zh]).start()
+            pltpu.make_async_copy(gx.at[ZH], gx.at[zh], gr.at[zh]).start()
+
+        @pl.when(jnp.logical_not(here))
+        def _():
+            remote(tok, xraw.at[zh], xs.at[k], xw.at[zh], dev(y, x, k, p, c)).start()
+            remote(gx.at[ZH], gx.at[zh], gs.at[k], gr.at[zh], dev(y, x, k, p, c)).start()
+
     arrived(st_z, n_z, st_r.at[0])
     st_xyc[xyc] = jnp.sum(st_z[...], axis=0)
     share(st_xyc, xyc, plane_peers, st_s.at[2], st_r.at[2])
@@ -169,22 +184,15 @@
     mean_col, inv_col = rows_to_columns(mean, inverse)
     normed[...] = (tok[...].astype(F32) - mean_col) * inv_col
     invc[...] = jnp.broadcast_to(inv_col, (HD, HD))
-    nin[...] = (normed[...] * gain[...].astype(F32).reshape(1, -1)).astype(BF16)
-
-    for k in range(ZH):
-        here = (x == y) & (zh == k)
-        dst = xc.at[0, zh * NC + c, y]
-        landed = xr.at[0, zh * NC + c, y]
-
-        @pl.when(here)
-        def _():
-            pltpu.make_async_copy(nin, dst, landed).start()
-            pltpu.make_async_copy(gx.at[ZH], gx.at[zh], gr.at[zh]).start()
-
-        @pl.when(jnp.logical_not(here))
-        def _():
-            remote(nin, dst, xs.at[k], landed, dev(y, x, k, p, c)).start()
-            remote(gx.at[ZH], gx.at[zh], gs.at[k], gr.at[zh], dev(y, x, k, p, c)).start()
+    mi[0] = jnp.concatenate([mean, inverse], axis=0)
+
+    @pl.when(x == y)
+    def _():
+        pltpu.make_async_copy(mi.at[0], mi.at[1], ms.at[0]).start()
+
+    @pl.when(x != y)
+    def _():
+        remote(mi.at[0], mi.at[1], ms.at[1], ms.at[0], dev(y, x, zh, p, c)).start()
 
     arrived(st_xyc, n_xyc, st_r.at[2])
     total = jnp.sum(st_xyc[...], axis=0)
@@ -234,10 +242,15 @@
         pltpu.make_async_copy(ref, ref, sem).wait()
 
     def send_tokens():
+        wait_block(mi.at[1], ms.at[0])
+        mean_there, inv_there = rows_to_columns(mi[1, 0:1], mi[1, 1:2])
         for k in range(ZH):
             j = k * NC + c
             block = xc.at[0, j, x]
-            wait_block(block, xr.at[0, j, x])
+            wait_block(xraw.at[k], xw.at[k])
+            wait_block(gx.at[k], gr.at[k])
+            hat = (xraw[k].astype(F32) - mean_there) * inv_there
+            xc[0, j, x] = (hat * gx[k, 0:1]).astype(BF16)
             for i, device in enumerate(near_peers):
                 remote(block, block, n3s.at[k, i], xr.at[0, j, x], device).start()
 
@@ -344,98 +357,105 @@
         for i, (_, device) in enumerate(y_peers):
             remote(dbuf.at[r, y], dbuf.at[r, y], ds_.at[r, i], dr.at[r, y], device).start()
 
-    def term_block(r, tb, own):
-        if not own:
+    goal = [1 - zh, zh]
+    apart = width // rows
+
+    def term_block(side, r, tb, wait):
+        if wait:
             wait_block(dbuf.at[r, tb], dr.at[r, tb])
-        for j in range(ZH * NC):
+        for half_c in range(NC):
+            j = goal[side] * NC + half_c
             acc = None
             for m in range(3):
-                weights = wall[m].reshape(ZL * rows, wall.shape[4])[j * width : (j + 1) * width]
+                weights = wall[m, pl.ds(j * apart, apart)].reshape(width, wall.shape[4])
                 term = mm_nt(dbuf[r, tb, m], weights)
                 acc = term if acc is None else acc + term
-            tbuf[j % NC, r, tb, j // NC] = acc.astype(BF16)
+            tbuf[half_c, side, r, tb] = acc.astype(BF16)
         remote(
-            tbuf.at[1 - c, r, tb], tr.at[r, tb], tcs.at[r, tb], tcr.at[r, tb], dev(x, y, zh, p, 1 - c)
+            tbuf.at[1 - c, side, r, tb], tr.at[side, r, tb], tcs.at[side, r, tb], tcr.at[side, r, tb], other_core
         ).start()
 
-    def add_cores(r, tb):
-        wait_block(tr.at[r, tb], tcr.at[r, tb])
-        sbuf[r, tb] = (tbuf[c, r, tb].astype(F32) + tr[r, tb].astype(F32)).astype(BF16)
+    def add_cores(side, r, tb):
+        wait_block(tr.at[side, r, tb], tcr.at[side, r, tb])
+        sbuf[side, r, tb] = (tbuf[c, side, r, tb].astype(F32) + tr[side, r, tb].astype(F32)).astype(BF16)
 
         @pl.when(tb != x)
         def _():
-            remote(sbuf.at[r, tb], sr.at[r, x], ss.at[r, tb], srs.at[r, x], dev(tb, y, zh, p, c)).start()
-
+            remote(
+                sbuf.at[side, r, tb], sr.at[side, r, x], ss.at[side, r, tb], srs.at[side, r, x], dev(tb, y, zh, p, c)
+            ).start()
+
+    other_core = dev(x, y, zh, p, 1 - c)
     order = [0, 1, 3, 2] if NY == 4 else list(range(NY))
-    for r in range(NR):
+
+    def blocks(side, r):
         before = None
         for i in order:
-            tb = lax.rem(y + i, NY)
-            term_block(r, tb, i == 0)
+            tb = at_y[i]
+            term_block(side, r, tb, side == 0 and i > 0)
             if before is not None:
-                add_cores(r, before)
+                add_cores(side, r, before)
             before = tb
-        add_cores(r, before)
-
-    for k in range(ZH):
-        wait_block(gx.at[k], gr.at[k])
-    firsts, seconds = [], []
+        add_cores(side, r, before)
+
+    firsts, seconds = [0.0] * NR, [0.0] * NR
+
+    def gather_x(side, r):
+        k = goal[side]
+        value = sbuf[side, r, x].astype(F32)
+        for i in range(1, NX):
+            wait_block(sr.at[side, r, at_x[i]], srs.at[side, r, at_x[i]])
+            value = value + sr[side, r, at_x[i]].astype(F32)
+        ubuf[side, r] = value.astype(BF16)
+        if side == 0:
+            remote(ubuf.at[0, r], ur.at[r, zh], us.at[0, r], urs.at[r, zh], dev(y, x, k, p, c)).start()
+        else:
+
+            @pl.when(x == y)
+            def _():
+                pltpu.make_async_copy(ubuf.at[1, r], ur.at[r, zh], urs.at[r, zh]).start()
+
+            @pl.when(x != y)
+            def _():
+                remote(ubuf.at[1, r], ur.at[r, zh], us.at[1, r], urs.at[r, zh], dev(y, x, k, p, c)).start()
+
+        tokens_in = xc[0, k * NC + c, x, r * half : (r + 1) * half].astype(F32)
+        firsts[r] = firsts[r] + jnp.sum(value * gx[k, 0:1], axis=-1, keepdims=True)
+        seconds[r] = seconds[r] + jnp.sum(value * tokens_in, axis=-1, keepdims=True)
+
     for r in range(NR):
-        value = sbuf[r, x].astype(F32)
-        for i in range(1, NX):
-            k = lax.rem(x + i, NX)
-            wait_block(sr.at[r, k], srs.at[r, k])
-            value = value + sr[r, k].astype(F32)
-        ubuf[r] = value.astype(BF16)
-        for k in range(ZH):
-            here = (x == y) & (zh == k)
-
-            @pl.when(here)
-            def _():
-                pltpu.make_async_copy(ubuf.at[r, k], ur.at[r, zh], urs.at[r, zh]).start()
-
-            @pl.when(jnp.logical_not(here))
-            def _():
-                remote(ubuf.at[r, k], ur.at[r, zh], us.at[r, k], urs.at[r, zh], dev(y, x, k, p, c)).start()
-
-        first, second = 0.0, 0.0
-        for k in range(ZH):
-            tokens_in = xc[0, k * NC + c, x, r * half : (r + 1) * half].astype(F32)
-            first = first + jnp.sum(value[k] * gx[k, 0:1], axis=-1, keepdims=True)
-            second = second + jnp.sum(value[k] * tokens_in, axis=-1, keepdims=True)
-        firsts.append(first)
-        seconds.append(second)
-    fa[zh] = columns_to_rows(jnp.concatenate(firsts, axis=0), jnp.concatenate(seconds, axis=0))[0:2]
-    share(fa, zh, [partner], st_s.at[3], st_r.at[3])
-    arrived(fa, ZH, st_r.at[3])
-    fb[NY * NC] = jnp.sum(fa[...], axis=0)
-    yc = y * NC + c
-
-    def send_sums(i, carry):
-        device = dev(lax.div(i, NC), x, zh, p, lax.rem(i, NC))
-        here = (x == y) & (i == xcore)
-
-        @pl.when(here)
-        def _():
-            pltpu.make_async_copy(fb.at[NY * NC], fb.at[yc], st_r.at[4]).start()
-
-        @pl.when(jnp.logical_not(here))
-        def _():
-            remote(fb.at[NY * NC], fb.at[yc], fs.at[i], st_r.at[4], device).start()
-
-        return carry
-
-    lax.fori_loop(0, NX * NC, send_sums, 0)
+        blocks(0, r)
     for r in range(NR):
-        for k in range(ZH):
-            wait_block(ur.at[r, k], urs.at[r, k])
-    arrived(fb, NY * NC + 1, st_r.at[4])
-    sums = jnp.sum(fb[0 : NY * NC], axis=0) * (1.0 / n_feat)
+        gather_x(0, r)
+        blocks(1, r)
+    for r in range(NR):
+        gather_x(1, r)
+    n_sums = NY * ZH * NC
+    fb[n_sums] = columns_to_rows(jnp.concatenate(firsts, axis=0), jnp.concatenate(seconds, axis=0))[0:2]
+    slot = (y * ZH + zh) * NC + c
+    for far in (1, 0):
+        for i in range(NX):
+            for q in range(NC):
+                device = dev(at_x[i], x, at_z[far], p, at_c[q])
+
+                @pl.when((x == y) & (far + i + q == 0))
+                def _():
+                    pltpu.make_async_copy(fb.at[n_sums], fb.at[slot], st_r.at[4]).start()
+
+                @pl.when((x != y) | (far + i + q > 0))
+                def _():
+                    remote(
+                        fb.at[n_sums], fb.at[slot], fs.at[(far * NX + i) * NC + q], st_r.at[4], device
+                    ).start()
+
+    arrived(fb, n_sums + 1, st_r.at[4])
+    sums = jnp.sum(fb[0:n_sums], axis=0) * (1.0 / n_feat)
     first, second = rows_to_columns(sums[0:1], sums[1:2])
     for r in range(NR):
         part = slice(r * half, (r + 1) * half)
-        share_sum = ur[r, 0].astype(F32)
-        for k in range(1, ZH):
+        share_sum = 0.0
+        for k in range(ZH):
+            wait_block(ur.at[r, k], urs.at[r, k])
             share_sum = share_sum + ur[r, k].astype(F32)
         upstream = share_sum * gain[...].astype(F32).reshape(1, -1)
         out[part] = ((upstream - first[part] - normed[part] * second[part]) * invc[part, 0:1]).astype(BF16)
@@ -443,16 +463,22 @@
     arrived(st_z, n_z, st_s.at[0])
     arrived(rs, n_mp, st_s.at[1])
     arrived(st_xyc, n_xyc, st_s.at[2])
-    arrived(fa, ZH, st_s.at[3])
     for k in range(ZH):
         here = (x == y) & (zh == k)
 
         @pl.when(jnp.logical_not(here))
         def _():
-            wait_block(nin, xs.at[k])
+            wait_block(xraw.at[0], xs.at[k])
             wait_block(gx.at[ZH], gs.at[k])
-            for r in range(NR):
-                wait_block(ubuf.at[r, k], us.at[r, k])
+
+    @pl.when(x != y)
+    def _():
+        wait_block(mi.at[0], ms.at[1])
+        for r in range(NR):
+            wait_block(ubuf.at[1, r], us.at[1, r])
+
+    for r in range(NR):
+        wait_block(ubuf.at[0, r], us.at[0, r])
 
     def left_y(i, carry):
         for j in range(ZH * NC):
@@ -465,28 +491,32 @@
 
     lax.fori_loop(0, NY - 1, left_y, 0)
 
-    def left_xc(i, carry):
-        @pl.when(i > 0)
-        def _():
-            for k in range(ZH):
-                wait_block(xc.at[0, 0, 0], n3s.at[k, i - 1])
-
-        @pl.when((x != y) | (i != xcore))
+    def left_near(i, carry):
+        for k in range(ZH):
+            wait_block(xc.at[0, 0, 0], n3s.at[k, i])
+        return carry
+
+    lax.fori_loop(0, NX * NC - 1, left_near, 0)
+
+    def left_sums(i, carry):
+        @pl.when((x != y) | (i > 0))
         def _():
             wait_block(fb.at[0], fs.at[i])
 
         return carry
 
-    lax.fori_loop(0, NX * NC, left_xc, 0)
+    lax.fori_loop(0, ZH * NX * NC, left_sums, 0)
 
     def left_blocks(tb, carry):
-        for r in range(NR):
-            wait_block(tr.at[r, tb], tcs.at[r, tb])
+        for side in range(2):
+            for r in range(NR):
+                wait_block(tr.at[side, r, tb], tcs.at[side, r, tb])
 
         @pl.when(tb != x)
         def _():
-            for r in range(NR):
-                wait_block(sbuf.at[r, tb], ss.at[r, tb])
+            for side in range(2):
+                for r in range(NR):
+                    wait_block(sbuf.at[side, r, tb], ss.at[side, r, tb])
 
         return carry
 
@@ -530,9 +560,9 @@
             pltpu.VMEM((NX * NY * NC, 1, HD), F32),
             pltpu.VMEM((n_mp, 2, HD), F32),
             pltpu.VMEM((ZH + 1, 8, width), F32),
-            pltpu.VMEM((ZH, 2, HD), F32),
-            pltpu.VMEM((NY * NC + 1, 2, HD), F32),
-            pltpu.VMEM((HD, width), BF16),
+            pltpu.VMEM((NY * ZH * NC + 1, 2, HD), F32),
+            pltpu.VMEM((2, 2, HD), F32),
+            pltpu.VMEM((ZH, HD, width), BF16),
             pltpu.VMEM((HD, width), F32),
             pltpu.VMEM((HD, HD), F32),
             pltpu.VMEM((2, nj, NY, HD, width), BF16),
@@ -542,18 +572,20 @@
             pltpu.VMEM((4, NY, HD, columns), BF16),
             pltpu.VMEM((4, NY, HD, columns), BF16),
             pltpu.VMEM((NR, NY, 3, HD // NR, columns), BF16),
-            pltpu.VMEM((NC, NR, NY, ZH, HD // NR, width), BF16),
-            pltpu.VMEM((NR, NY, ZH, HD // NR, width), BF16),
-            pltpu.VMEM((NR, NY, ZH, HD // NR, width), BF16),
-            pltpu.VMEM((NR, NX, ZH, HD // NR, width), BF16),
-            pltpu.VMEM((NR, ZH, HD // NR, width), BF16),
+            pltpu.VMEM((NC, 2, NR, NY, HD // NR, width), BF16),
+            pltpu.VMEM((2, NR, NY, HD // NR, width), BF16),
+            pltpu.VMEM((2, NR, NY, HD // NR, width), BF16),
+            pltpu.VMEM((2, NR, NX, HD // NR, width), BF16),
+            pltpu.VMEM((2, NR, HD // NR, width), BF16),
             pltpu.VMEM((NR, ZH, HD // NR, width), BF16),
             dma((4,)),
             dma((4,)),
             dma((5,)),
             dma((ZH,)),
             dma((ZH,)),
-            dma((NX * NC,)),
+            dma((ZH * NX * NC,)),
+            dma((2,)),
+            dma((ZH,)),
             dma((ZH,)),
             dma((2, nj, NY)),
             dma((NY, nj)),
@@ -564,11 +596,11 @@
             dma((4, NY)),
             dma((NR, NY)),
             dma((NR, NY)),
-            dma((NR, NY)),
-            dma((NR, NY)),
-            dma((NR, NY)),
-            dma((NR, NX)),
-            dma((NR, ZH)),
+            dma((2, NR, NY)),
+            dma((2, NR, NY)),
+            dma((2, NR, NY)),
+            dma((2, NR, NX)),
+            dma((2, NR)),
             dma((NR, ZH)),
         ],
         compiler_params=pltpu.CompilerParams(

time: 148 us -> 145 us (0.980)
  Pallas kernels: 146 us -> 142 us
    pallas_call x1, Pallas kernels: 146 us -> 142 us  [per_device(): pl.pallas_call(kernel, out_shape=jax.ShapeDtypeStruct((HD, width), BF16),...]
where the time goes in v4:
time: 145 us; the launch traced here: 144 us
  Pallas kernels  142 us (98%)
  local copies, waits for them, and re-layouts  1.54 us (1%)
    pallas_call x1, Pallas kernels, per_device(): pl.pallas_call(kernel, out_shape=jax.ShapeDtypeStruct((HD, width), BF16),...  142 us

profile of v4, /device:TPU:7, one launch (start us, length us, event | category | flops | bytes accessed | tf_op | source)
XLA Modules:
  0.0 143.6 jit_solution(782797082381592158)
XLA Ops:
  0.0 142.1 %shard_map.55 = bf16[128,384]{1,0:T(8,128)(2,1)} custom-call(bf16[128,384]{1,0:T(8,128)(2,1)} %tok_hbm.1, bf16[384]{0:T(512)(128)(2,1)} %gain_hbm.1, bf16[4,192,256]{2,1,0:T(8,128)(2,1)} %w_hbm.1, bf16[4,192,256]{2,1,0:T(8,128)(2,1)} %g_hbm.1, bf16[128,6144]{1,0:T(8,128)(2,1)} %cot.1), custom_call_target="tpu_custom_call" | custom-call | tf_op jit(solution)/shard_map/pallas_call | solution.py:549
  142.1 1.5 %copy.7 = bf16[128,384]{1,0:T(8,128)(2,1)} copy(bf16[128,384]{1,0:T(8,128)(2,1)} %shard_map.55) | data formatting | bytes 196608

commit v5 on v4

--- a/solution.py
+++ b/solution.py
@@ -10,6 +10,7 @@
 HD = 128
 NX, NY, ZH, ZL, NC = 4, 4, 2, 8, 2
 NH = 2
+EXTRA = 16
 NR = 2
 ascent_radius = 0.15
 
@@ -54,8 +55,8 @@
 def kernel(
     tok_hbm, gain_hbm, w_hbm, g_hbm, cot, out,
     tok, gain, w, g,
-    st_z, st_xyc, rs, gx, fb, mi, xraw, normed, invc, xc, wall, pf, pown, psend, precv, dbuf, tbuf, tr, sbuf, sr, ubuf, ur,
-    ins, st_s, st_r, gs, gr, fs, ms, xs, xw, xr, cs, n3s, ws, wr, ps, pr, ds_, dr, tcs, tcr, ss, srs, us, urs,
+    st_z, st_xyc, rs, gx, fin, mi, xraw, normed, invc, xc, wall, pf, pown, psend, precv, dbuf, tbuf, tr, sbuf, sr, ubuf, ur,
+    ins, st_s, st_r, gs, gr, ms, xs, xw, xr, cs, n3s, ws, wr, ps, pr, ds_, dr, tcs, tcr, ss, srs, us, urs,
 ):
     n_mp = NX * ZH * NC
     n_z = ZH * ZL
@@ -87,6 +88,9 @@
         return pltpu.make_async_remote_copy(
             src_ref=src, dst_ref=dst, send_sem=ssem, recv_sem=rsem, device_id=device, device_id_type=MESH
         )
+
+    def token_rows(sel, j, tb):
+        return xc.at[sel, j, pl.ds(pl.multiple_of(tb * HD, HD), HD)]
 
     def share(buf, mine, peers, ssem, rsem):
         for device in peers:
@@ -127,13 +131,10 @@
         greet(device)
     for device in far_peers + plane_peers:
         greet(device)
-    for j in range(1, NY):
-        for i in range(NX):
-
-            @pl.when((at_y[j] == x) | (at_x[i] == y))
-            def _():
-                for q in range(NC):
-                    greet(dev(at_x[i], at_y[j], 1 - zh, p, at_c[q]))
+
+    @pl.when(x != y)
+    def _():
+        greet(dev(y, x, 1 - zh, p, c))
 
     loads[0].wait()
     loads[1].wait()
@@ -151,30 +152,30 @@
     part_mean = jnp.sum(part, axis=-1, keepdims=True) * (1.0 / width)
     part_square = jnp.sum(jnp.square(part - part_mean), axis=-1, keepdims=True)
     rs[mp] = columns_to_rows(part_mean, part_square)[0:2]
-    gx_row = jnp.broadcast_to(gain[...].astype(F32).reshape(1, -1), (8, width))
-    gx[ZH] = gx_row
-
-    far_places = jnp.where(x == y, 2 * NX - 1, 3 * NX - 2)
-    pl.semaphore_wait(barrier, (n_z - 1) + (n_xyc - 1) + NC * far_places - 1)
+    gx[ZH * NC] = gain[...].astype(F32).reshape(1, -1)
+    for j in range(ZH * NC):
+        xc[1, j, NY * HD :] = jnp.zeros((EXTRA, width), BF16)
+
+    pl.semaphore_wait(
+        barrier, (n_z - 1) + (n_xyc - 1) + (ZH - 1) * (NX * NC - 1) + jnp.where(x != y, ZH - 1, 0)
+    )
 
     share(st_z, z, [d for _, d in z_peers], st_s.at[0], st_r.at[0])
     share(rs, mp, near_peers + [partner] + far_peers, st_s.at[1], st_r.at[1])
+    arrived(st_z, n_z, st_r.at[0])
+    st_xyc[xyc] = jnp.sum(st_z[...], axis=0)
+    share(st_xyc, xyc, plane_peers, st_s.at[2], st_r.at[2])
+
     for k in at_z[::-1]:
         here = (x == y) & (zh == k)
 
         @pl.when(here)
         def _():
             pltpu.make_async_copy(tok, xraw.at[zh], xw.at[zh]).start()
-            pltpu.make_async_copy(gx.at[ZH], gx.at[zh], gr.at[zh]).start()
 
         @pl.when(jnp.logical_not(here))
         def _():
             remote(tok, xraw.at[zh], xs.at[k], xw.at[zh], dev(y, x, k, p, c)).start()
-            remote(gx.at[ZH], gx.at[zh], gs.at[k], gr.at[zh], dev(y, x, k, p, c)).start()
-
-    arrived(st_z, n_z, st_r.at[0])
-    st_xyc[xyc] = jnp.sum(st_z[...], axis=0)
-    share(st_xyc, xyc, plane_peers, st_s.at[2], st_r.at[2])
 
     arrived(rs, n_mp, st_r.at[1])
     means = rs[:, 0:1, :]
@@ -223,16 +224,25 @@
 
     send_own(0)
 
+    mp_peers = near_peers + [partner] + far_peers
+
+    @pl.when(x == y)
+    def _():
+        slot = zh * NC + c
+        pltpu.make_async_copy(gx.at[ZH * NC], gx.at[slot], gr.at[0]).start()
+        for i, device in enumerate(mp_peers):
+            remote(gx.at[ZH * NC], gx.at[slot], gs.at[i], gr.at[0], device).start()
+
     for j in range(ZH * NC):
         pltpu.make_async_copy(
-            cot.at[:, pl.ds(pl.multiple_of(y * band + j * width, HD), width)], xc.at[1, j, y], xr.at[1, j, y]
+            cot.at[:, pl.ds(pl.multiple_of(y * band + j * width, HD), width)], token_rows(1, j, y), xr.at[1, j, y]
         ).start()
 
     for i, (k, device) in enumerate(y_peers):
         for j in range(ZH * NC):
             remote(
                 cot.at[:, pl.ds(pl.multiple_of(k * band + j * width, HD), width)],
-                xc.at[1, j, y],
+                token_rows(1, j, y),
                 cs.at[i, j],
                 xr.at[1, j, y],
                 device,
@@ -243,14 +253,16 @@
 
     def send_tokens():
         wait_block(mi.at[1], ms.at[0])
+        arrived(gx, ZH * NC + 1, gr.at[0])
+        for j in range(ZH * NC):
+            xc[0, j, NY * HD :] = jnp.broadcast_to(gx[j], (EXTRA, width)).astype(BF16)
         mean_there, inv_there = rows_to_columns(mi[1, 0:1], mi[1, 1:2])
         for k in range(ZH):
             j = k * NC + c
-            block = xc.at[0, j, x]
+            block = token_rows(0, j, x)
             wait_block(xraw.at[k], xw.at[k])
-            wait_block(gx.at[k], gr.at[k])
             hat = (xraw[k].astype(F32) - mean_there) * inv_there
-            xc[0, j, x] = (hat * gx[k, 0:1]).astype(BF16)
+            block[...] = (hat * gx[j]).astype(BF16)
             for i, device in enumerate(near_peers):
                 remote(block, block, n3s.at[k, i], xr.at[0, j, x], device).start()
 
@@ -262,7 +274,7 @@
 
                 @pl.when((sel == 1) | (lax.rem(j, NC) != c) | (tb != x))
                 def _():
-                    wait_block(xc.at[sel, j, tb], xr.at[sel, j, tb])
+                    wait_block(token_rows(sel, j, tb), xr.at[sel, j, tb])
 
                 return carry
 
@@ -272,10 +284,11 @@
         weights = wall[m].reshape(ZL * rows, columns)
         acc = None
         for j in range(ZH * NC):
-            left = xc[sel, j].reshape(NY * HD, width)
-            term = mm(left, weights[j * width : (j + 1) * width])
+            term = mm(xc[sel, j], weights[j * width : (j + 1) * width])
             acc = term if acc is None else acc + term
-        pf[...] = acc.reshape(NY, HD, columns)
+        for k in range(NY):
+            pf[k, 0:HD] = acc[k * HD : (k + 1) * HD]
+            pf[k, HD:] = acc[NY * HD :]
         pown[m] = pf[y]
         psend[m] = pf[...].astype(BF16)
         for i, (k, device) in enumerate(y_peers):
@@ -326,10 +339,11 @@
             value = value + precv[m, k].astype(F32)
         return value
 
-    grad_attn_all = projected(3).astype(BF16)
-    query_all = projected(0)
-    key_all = projected(1)
-    value_all = projected(2).astype(BF16)
+    grad_attn_all = projected(3)[0:HD].astype(BF16)
+    whole = [projected(m) for m in range(3)]
+    query_all, key_all = whole[0][0:HD], whole[1][0:HD]
+    value_all = whole[2][0:HD].astype(BF16)
+    first_col, second_col = 0.0, 0.0
     score_scale = HD ** (-0.5)
     for h in range(wall.shape[4] // HD):
         cols = slice(h * HD, (h + 1) * HD)
@@ -351,11 +365,18 @@
             grad_values.astype(BF16),
         )
         for m in range(3):
+            grad = grads[m].astype(F32)
+            first_col = first_col + jnp.sum(grad * whole[m][HD : HD + 1, cols], axis=-1, keepdims=True)
+            second_col = second_col + jnp.sum(grad * whole[m][0:HD, cols], axis=-1, keepdims=True)
+        for m in range(3):
             for r in range(NR):
                 dbuf[r, y, m, :, cols] = grads[m][r * half : (r + 1) * half]
     for r in range(NR):
         for i, (_, device) in enumerate(y_peers):
             remote(dbuf.at[r, y], dbuf.at[r, y], ds_.at[r, i], dr.at[r, y], device).start()
+
+    fin[mp] = columns_to_rows(first_col, second_col)[0:2]
+    share(fin, mp, near_peers + [partner] + far_peers, st_s.at[3], st_r.at[3])
 
     goal = [1 - zh, zh]
     apart = width // rows
@@ -398,8 +419,6 @@
             before = tb
         add_cores(side, r, before)
 
-    firsts, seconds = [0.0] * NR, [0.0] * NR
-
     def gather_x(side, r):
         k = goal[side]
         value = sbuf[side, r, x].astype(F32)
@@ -419,10 +438,6 @@
             def _():
                 remote(ubuf.at[1, r], ur.at[r, zh], us.at[1, r], urs.at[r, zh], dev(y, x, k, p, c)).start()
 
-        tokens_in = xc[0, k * NC + c, x, r * half : (r + 1) * half].astype(F32)
-        firsts[r] = firsts[r] + jnp.sum(value * gx[k, 0:1], axis=-1, keepdims=True)
-        seconds[r] = seconds[r] + jnp.sum(value * tokens_in, axis=-1, keepdims=True)
-
     for r in range(NR):
         blocks(0, r)
     for r in range(NR):
@@ -430,26 +445,8 @@
         blocks(1, r)
     for r in range(NR):
         gather_x(1, r)
-    n_sums = NY * ZH * NC
-    fb[n_sums] = columns_to_rows(jnp.concatenate(firsts, axis=0), jnp.concatenate(seconds, axis=0))[0:2]
-    slot = (y * ZH + zh) * NC + c
-    for far in (1, 0):
-        for i in range(NX):
-            for q in range(NC):
-                device = dev(at_x[i], x, at_z[far], p, at_c[q])
-
-                @pl.when((x == y) & (far + i + q == 0))
-                def _():
-                    pltpu.make_async_copy(fb.at[n_sums], fb.at[slot], st_r.at[4]).start()
-
-                @pl.when((x != y) | (far + i + q > 0))
-                def _():
-                    remote(
-                        fb.at[n_sums], fb.at[slot], fs.at[(far * NX + i) * NC + q], st_r.at[4], device
-                    ).start()
-
-    arrived(fb, n_sums + 1, st_r.at[4])
-    sums = jnp.sum(fb[0:n_sums], axis=0) * (1.0 / n_feat)
+    arrived(fin, n_mp, st_r.at[3])
+    sums = jnp.sum(fin[...], axis=0) * (1.0 / n_feat)
     first, second = rows_to_columns(sums[0:1], sums[1:2])
     for r in range(NR):
         part = slice(r * half, (r + 1) * half)
@@ -463,13 +460,13 @@
     arrived(st_z, n_z, st_s.at[0])
     arrived(rs, n_mp, st_s.at[1])
     arrived(st_xyc, n_xyc, st_s.at[2])
+    arrived(fin, n_mp, st_s.at[3])
     for k in range(ZH):
         here = (x == y) & (zh == k)
 
         @pl.when(jnp.logical_not(here))
         def _():
             wait_block(xraw.at[0], xs.at[k])
-            wait_block(gx.at[ZH], gs.at[k])
 
     @pl.when(x != y)
     def _():
@@ -482,7 +479,7 @@
 
     def left_y(i, carry):
         for j in range(ZH * NC):
-            wait_block(xc.at[1, j, 0], cs.at[i, j])
+            wait_block(token_rows(1, j, 0), cs.at[i, j])
         for m in range(4):
             wait_block(psend.at[m, 0], ps.at[m, i])
         for r in range(NR):
@@ -493,19 +490,15 @@
 
     def left_near(i, carry):
         for k in range(ZH):
-            wait_block(xc.at[0, 0, 0], n3s.at[k, i])
+            wait_block(token_rows(0, 0, 0), n3s.at[k, i])
         return carry
 
     lax.fori_loop(0, NX * NC - 1, left_near, 0)
 
-    def left_sums(i, carry):
-        @pl.when((x != y) | (i > 0))
-        def _():
-            wait_block(fb.at[0], fs.at[i])
-
-        return carry
-
-    lax.fori_loop(0, ZH * NX * NC, left_sums, 0)
+    @pl.when(x == y)
+    def _():
+        for i in range(n_mp - 1):
+            wait_block(gx.at[0], gs.at[i])
 
     def left_blocks(tb, carry):
         for side in range(2):
@@ -559,18 +552,18 @@
             pltpu.VMEM((ZH * ZL, 1, HD), F32),
             pltpu.VMEM((NX * NY * NC, 1, HD), F32),
             pltpu.VMEM((n_mp, 2, HD), F32),
-            pltpu.VMEM((ZH + 1, 8, width), F32),
-            pltpu.VMEM((NY * ZH * NC + 1, 2, HD), F32),
+            pltpu.VMEM((ZH * NC + 1, 1, width), F32),
+            pltpu.VMEM((n_mp, 2, HD), F32),
             pltpu.VMEM((2, 2, HD), F32),
             pltpu.VMEM((ZH, HD, width), BF16),
             pltpu.VMEM((HD, width), F32),
             pltpu.VMEM((HD, HD), F32),
-            pltpu.VMEM((2, nj, NY, HD, width), BF16),
+            pltpu.VMEM((2, nj, NY * HD + EXTRA, width), BF16),
             pltpu.VMEM((4, ZL, NH, rows // NH, columns), BF16),
-            pltpu.VMEM((NY, HD, columns), F32),
-            pltpu.VMEM((4, HD, columns), F32),
-            pltpu.VMEM((4, NY, HD, columns), BF16),
-            pltpu.VMEM((4, NY, HD, columns), BF16),
+            pltpu.VMEM((NY, HD + EXTRA, columns), F32),
+            pltpu.VMEM((4, HD + EXTRA, columns), F32),
+            pltpu.VMEM((4, NY, HD + EXTRA, columns), BF16),
+            pltpu.VMEM((4, NY, HD + EXTRA, columns), BF16),
             pltpu.VMEM((NR, NY, 3, HD // NR, columns), BF16),
             pltpu.VMEM((NC, 2, NR, NY, HD // NR, width), BF16),
             pltpu.VMEM((2, NR, NY, HD // NR, width), BF16),
@@ -580,10 +573,9 @@
             pltpu.VMEM((NR, ZH, HD // NR, width), BF16),
             dma((4,)),
             dma((4,)),
-            dma((5,)),
-            dma((ZH,)),
-            dma((ZH,)),
-            dma((ZH * NX * NC,)),
+            dma((4,)),
+            dma((n_mp - 1,)),
+            dma((1,)),
             dma((2,)),
             dma((ZH,)),
             dma((ZH,)),

time: 145 us -> 143 us (0.986)
  no operation moved by 1% of the time
where the time goes in v5:
time: 143 us
  Pallas kernels  141 us (99%)
  local copies, waits for them, and re-layouts  1.54 us (1%)
    pallas_call x1, Pallas kernels, per_device(): pl.pallas_call(kernel, out_shape=jax.ShapeDtypeStruct((HD, width), BF16),...  141 us

profile of v5, /device:TPU:7, one launch (start us, length us, event | category | flops | bytes accessed | tf_op | source)
XLA Modules:
  0.0 142.6 jit_solution(16189857255682483680)
XLA Ops:
  0.0 141.0 %shard_map.55 = bf16[128,384]{1,0:T(8,128)(2,1)} custom-call(bf16[128,384]{1,0:T(8,128)(2,1)} %tok_hbm.1, bf16[384]{0:T(512)(128)(2,1)} %gain_hbm.1, bf16[4,192,256]{2,1,0:T(8,128)(2,1)} %w_hbm.1, bf16[4,192,256]{2,1,0:T(8,128)(2,1)} %g_hbm.1, bf16[128,6144]{1,0:T(8,128)(2,1)} %cot.1), custom_call_target="tpu_custom_call" | custom-call | tf_op jit(solution)/shard_map/pallas_call | solution.py:542
  141.0 1.5 %copy.7 = bf16[128,384]{1,0:T(8,128)(2,1)} copy(bf16[128,384]{1,0:T(8,128)(2,1)} %shard_map.55) | data formatting | bytes 196608

commit v6 on v5

--- a/solution.py
+++ b/solution.py
@@ -343,7 +343,6 @@
     whole = [projected(m) for m in range(3)]
     query_all, key_all = whole[0][0:HD], whole[1][0:HD]
     value_all = whole[2][0:HD].astype(BF16)
-    first_col, second_col = 0.0, 0.0
     score_scale = HD ** (-0.5)
     for h in range(wall.shape[4] // HD):
         cols = slice(h * HD, (h + 1) * HD)
@@ -365,17 +364,20 @@
             grad_values.astype(BF16),
         )
         for m in range(3):
-            grad = grads[m].astype(F32)
-            first_col = first_col + jnp.sum(grad * whole[m][HD : HD + 1, cols], axis=-1, keepdims=True)
-            second_col = second_col + jnp.sum(grad * whole[m][0:HD, cols], axis=-1, keepdims=True)
-        for m in range(3):
             for r in range(NR):
                 dbuf[r, y, m, :, cols] = grads[m][r * half : (r + 1) * half]
     for r in range(NR):
         for i, (_, device) in enumerate(y_peers):
             remote(dbuf.at[r, y], dbuf.at[r, y], ds_.at[r, i], dr.at[r, y], device).start()
 
-    fin[mp] = columns_to_rows(first_col, second_col)[0:2]
+    first_part, second_part = 0.0, 0.0
+    for m in range(3):
+        grad = jnp.concatenate([dbuf[r, y, m].astype(F32) for r in range(NR)], axis=0)
+        first_part = first_part + grad * whole[m][HD : HD + 1]
+        second_part = second_part + grad * whole[m][0:HD]
+    fin[mp] = columns_to_rows(
+        jnp.sum(first_part, axis=-1, keepdims=True), jnp.sum(second_part, axis=-1, keepdims=True)
+    )[0:2]
     share(fin, mp, near_peers + [partner] + far_peers, st_s.at[3], st_r.at[3])
 
     goal = [1 - zh, zh]
@@ -411,13 +413,19 @@
 
     def blocks(side, r):
         before = None
-        for i in order:
+        for i in order[1:]:
             tb = at_y[i]
-            term_block(side, r, tb, side == 0 and i > 0)
+            term_block(side, r, tb, side == 0)
             if before is not None:
                 add_cores(side, r, before)
             before = tb
         add_cores(side, r, before)
+
+    own = [(side, r) for side in range(2) for r in range(NR)]
+    for side, r in own:
+        term_block(side, r, y, False)
+    for side, r in own:
+        add_cores(side, r, y)
 
     def gather_x(side, r):
         k = goal[side]
@@ -445,6 +453,75 @@
         blocks(1, r)
     for r in range(NR):
         gather_x(1, r)
+    arrived(st_z, n_z, st_s.at[0])
+    arrived(rs, n_mp, st_s.at[1])
+    arrived(st_xyc, n_xyc, st_s.at[2])
+    arrived(fin, n_mp, st_s.at[3])
+    for k in range(ZH):
+        here = (x == y) & (zh == k)
+
+        @pl.when(jnp.logical_not(here))
+        def _():
+            wait_block(xraw.at[0], xs.at[k])
+
+    @pl.when(x != y)
+    def _():
+        wait_block(mi.at[0], ms.at[1])
+
+    def left_y(i, carry):
+        for j in range(ZH * NC):
+            wait_block(token_rows(1, j, 0), cs.at[i, j])
+        for m in range(4):
+            wait_block(psend.at[m, 0], ps.at[m, i])
+        for r in range(NR):
+            wait_block(dbuf.at[r, 0], ds_.at[r, i])
+        return carry
+
+    lax.fori_loop(0, NY - 1, left_y, 0)
+
+    def left_near(i, carry):
+        for k in range(ZH):
+            wait_block(token_rows(0, 0, 0), n3s.at[k, i])
+        return carry
+
+    lax.fori_loop(0, NX * NC - 1, left_near, 0)
+
+    @pl.when(x == y)
+    def _():
+        for i in range(n_mp - 1):
+            wait_block(gx.at[0], gs.at[i])
+
+    def left_blocks(tb, carry):
+        for side in range(2):
+            for r in range(NR):
+                wait_block(tr.at[side, r, tb], tcs.at[side, r, tb])
+
+        @pl.when(tb != x)
+        def _():
+            for side in range(2):
+                for r in range(NR):
+                    wait_block(sbuf.at[side, r, tb], ss.at[side, r, tb])
+
+        return carry
+
+    lax.fori_loop(0, NY, left_blocks, 0)
+
+    def left_weights(i, carry):
+        m, s = lax.div(i, ZL), lax.rem(i, ZL)
+        for h in range(NH):
+
+            @pl.when((p < ZL - 1) & (s <= p))
+            def _():
+                wait_block(wall.at[m, s, h], ws.at[0, m, s, h])
+
+            @pl.when((p > 0) & (s >= p))
+            def _():
+                wait_block(wall.at[m, s, h], ws.at[1, m, s, h])
+
+        return carry
+
+    lax.fori_loop(0, 4 * ZL, left_weights, 0)
+
     arrived(fin, n_mp, st_r.at[3])
     sums = jnp.sum(fin[...], axis=0) * (1.0 / n_feat)
     first, second = rows_to_columns(sums[0:1], sums[1:2])
@@ -457,79 +534,12 @@
         upstream = share_sum * gain[...].astype(F32).reshape(1, -1)
         out[part] = ((upstream - first[part] - normed[part] * second[part]) * invc[part, 0:1]).astype(BF16)
 
-    arrived(st_z, n_z, st_s.at[0])
-    arrived(rs, n_mp, st_s.at[1])
-    arrived(st_xyc, n_xyc, st_s.at[2])
-    arrived(fin, n_mp, st_s.at[3])
-    for k in range(ZH):
-        here = (x == y) & (zh == k)
-
-        @pl.when(jnp.logical_not(here))
-        def _():
-            wait_block(xraw.at[0], xs.at[k])
-
-    @pl.when(x != y)
-    def _():
-        wait_block(mi.at[0], ms.at[1])
+    for side in range(2):
         for r in range(NR):
-            wait_block(ubuf.at[1, r], us.at[1, r])
-
-    for r in range(NR):
-        wait_block(ubuf.at[0, r], us.at[0, r])
-
-    def left_y(i, carry):
-        for j in range(ZH * NC):
-            wait_block(token_rows(1, j, 0), cs.at[i, j])
-        for m in range(4):
-            wait_block(psend.at[m, 0], ps.at[m, i])
-        for r in range(NR):
-            wait_block(dbuf.at[r, 0], ds_.at[r, i])
-        return carry
-
-    lax.fori_loop(0, NY - 1, left_y, 0)
-
-    def left_near(i, carry):
-        for k in range(ZH):
-            wait_block(token_rows(0, 0, 0), n3s.at[k, i])
-        return carry
-
-    lax.fori_loop(0, NX * NC - 1, left_near, 0)
-
-    @pl.when(x == y)
-    def _():
-        for i in range(n_mp - 1):
-            wait_block(gx.at[0], gs.at[i])
-
-    def left_blocks(tb, carry):
-        for side in range(2):
-            for r in range(NR):
-                wait_block(tr.at[side, r, tb], tcs.at[side, r, tb])
-
-        @pl.when(tb != x)
-        def _():
-            for side in range(2):
-                for r in range(NR):
-                    wait_block(sbuf.at[side, r, tb], ss.at[side, r, tb])
-
-        return carry
-
-    lax.fori_loop(0, NY, left_blocks, 0)
-
-    def left_weights(i, carry):
-        m, s = lax.div(i, ZL), lax.rem(i, ZL)
-        for h in range(NH):
-
-            @pl.when((p < ZL - 1) & (s <= p))
+
+            @pl.when((side == 0) | (x != y))
             def _():
-                wait_block(wall.at[m, s, h], ws.at[0, m, s, h])
-
-            @pl.when((p > 0) & (s >= p))
-            def _():
-                wait_block(wall.at[m, s, h], ws.at[1, m, s, h])
-
-        return carry
-
-    lax.fori_loop(0, 4 * ZL, left_weights, 0)
+                wait_block(ubuf.at[side, r], us.at[side, r])
 
 
 def per_device(tokens, norm_gain, attn_weights, stored_grads, cotangent):

time: 143 us -> 140 us (0.979)
  Pallas kernels: 141 us -> 139 us
    pallas_call x1, Pallas kernels: 141 us -> 139 us  [per_device(): pl.pallas_call(kernel, out_shape=jax.ShapeDtypeStruct((HD, width), BF16),...]
where the time goes in v6:
time: 140 us
  Pallas kernels  139 us (99%)
  local copies, waits for them, and re-layouts  1.54 us (1%)
    pallas_call x1, Pallas kernels, per_device(): pl.pallas_call(kernel, out_shape=jax.ShapeDtypeStruct((HD, width), BF16),...  139 us

profile of v6, /device:TPU:7, one launch (start us, length us, event | category | flops | bytes accessed | tf_op | source)
XLA Modules:
  0.0 140.1 jit_solution(14583332768741120784)
XLA Ops:
  0.0 138.6 %shard_map.55 = bf16[128,384]{1,0:T(8,128)(2,1)} custom-call(bf16[128,384]{1,0:T(8,128)(2,1)} %tok_hbm.1, bf16[384]{0:T(512)(128)(2,1)} %gain_hbm.1, bf16[4,192,256]{2,1,0:T(8,128)(2,1)} %w_hbm.1, bf16[4,192,256]{2,1,0:T(8,128)(2,1)} %g_hbm.1, bf16[128,6144]{1,0:T(8,128)(2,1)} %cot.1), custom_call_target="tpu_custom_call" | custom-call | tf_op jit(solution)/shard_map/pallas_call | solution.py:552
  138.6 1.5 %copy.7 = bf16[128,384]{1,0:T(8,128)(2,1)} copy(bf16[128,384]{1,0:T(8,128)(2,1)} %shard_map.55) | data formatting | bytes 196608

commit v7 on v6

--- a/solution.py
+++ b/solution.py
@@ -446,11 +446,14 @@
             def _():
                 remote(ubuf.at[1, r], ur.at[r, zh], us.at[1, r], urs.at[r, zh], dev(y, x, k, p, c)).start()
 
-    for r in range(NR):
+    for r in range(NR - 1):
         blocks(0, r)
-    for r in range(NR):
         gather_x(0, r)
+    blocks(0, NR - 1)
+    for r in range(NR - 1):
         blocks(1, r)
+    gather_x(0, NR - 1)
+    blocks(1, NR - 1)
     for r in range(NR):
         gather_x(1, r)
     arrived(st_z, n_z, st_s.at[0])

time: 140 us -> 142 us (1.014)
  Pallas kernels: 139 us -> 141 us
    pallas_call x1, Pallas kernels: 139 us -> 141 us  [per_device(): pl.pallas_call(kernel, out_shape=jax.ShapeDtypeStruct((HD, width), BF16),...]
where the time goes in v7:
time: 142 us
  Pallas kernels  141 us (99%)
  local copies, waits for them, and re-layouts  1.54 us (1%)
    pallas_call x1, Pallas kernels, per_device(): pl.pallas_call(kernel, out_shape=jax.ShapeDtypeStruct((HD, width), BF16),...  141 us

profile of v7, /device:TPU:7, one launch (start us, length us, event | category | flops | bytes accessed | tf_op | source)
XLA Modules:
  0.0 142.1 jit_solution(2704506343734053285)
XLA Ops:
  0.0 140.6 %shard_map.55 = bf16[128,384]{1,0:T(8,128)(2,1)} custom-call(bf16[128,384]{1,0:T(8,128)(2,1)} %tok_hbm.1, bf16[384]{0:T(512)(128)(2,1)} %gain_hbm.1, bf16[4,192,256]{2,1,0:T(8,128)(2,1)} %w_hbm.1, bf16[4,192,256]{2,1,0:T(8,128)(2,1)} %g_hbm.1, bf16[128,6144]{1,0:T(8,128)(2,1)} %cot.1), custom_call_target="tpu_custom_call" | custom-call | tf_op jit(solution)/shard_map/pallas_call | solution.py:555
  140.6 1.5 %copy.7 = bf16[128,384]{1,0:T(8,128)(2,1)} copy(bf16[128,384]{1,0:T(8,128)(2,1)} %shard_map.55) | data formatting | bytes 196608

commit v8 on v6

--- a/solution.py
+++ b/solution.py
@@ -450,6 +450,7 @@
         blocks(0, r)
     for r in range(NR):
         gather_x(0, r)
+    for r in range(NR):
         blocks(1, r)
     for r in range(NR):
         gather_x(1, r)

time: 140 us -> 141 us (level)
  no operation moved by 1% of the time
where the time goes in v8:
time: 141 us
  Pallas kernels  140 us (99%)
  local copies, waits for them, and re-layouts  1.54 us (1%)
    pallas_call x1, Pallas kernels, per_device(): pl.pallas_call(kernel, out_shape=jax.ShapeDtypeStruct((HD, width), BF16),...  140 us

profile of v8, /device:TPU:7, one launch (start us, length us, event | category | flops | bytes accessed | tf_op | source)
XLA Modules:
  0.0 141.3 jit_solution(693479848301549368)
XLA Ops:
  0.0 139.7 %shard_map.55 = bf16[128,384]{1,0:T(8,128)(2,1)} custom-call(bf16[128,384]{1,0:T(8,128)(2,1)} %tok_hbm.1, bf16[384]{0:T(512)(128)(2,1)} %gain_hbm.1, bf16[4,192,256]{2,1,0:T(8,128)(2,1)} %w_hbm.1, bf16[4,192,256]{2,1,0:T(8,128)(2,1)} %g_hbm.1, bf16[128,6144]{1,0:T(8,128)(2,1)} %cot.1), custom_call_target="tpu_custom_call" | custom-call | tf_op jit(solution)/shard_map/pallas_call | solution.py:553
  139.7 1.5 %copy.7 = bf16[128,384]{1,0:T(8,128)(2,1)} copy(bf16[128,384]{1,0:T(8,128)(2,1)} %shard_map.55) | data formatting | bytes 196608
